TPU v7x, 256 devices: a whole 4x4x8 slice. The times are simulated.
256 devices in a mesh: pts: 16 (over x, y_lo, core), lst: 16 (over z, y_hi).
Axes of the slice: x: 4, y: 4 (y_hi: 2, y_lo: 2; y = y_hi * 2 + y_lo), z: 8, core: 2. Of those that a mesh axis runs over, the one named last changes fastest.
Arguments:
- tower_out: bfloat16 [32768, 1024], P('pts', 'lst'), may hold values from -6 to 6
- projection: bfloat16 [1024, 256], P('lst'), may hold values from -1 to 1
- centroids: bfloat16 [16384, 256], P('lst'), may hold values from -6 to 6
Outputs:
- new_centroids: float32 [16384, 256], P(('lst', 'pts'))
- row_log: float32 [32768], P('pts')
All inputs are finite; a program needn't handle non-finite values.
Results may differ from a plain program's by a relative error of at most 0.0045.
Values may be sent and summed in bfloat16 or wider, within the bound.
No kernel may reach another device: no remote copies, remote signals or barrier semaphores. Data moves between devices by JAX's collectives and lax.ppermute only.
A program may use at most 64 MiB of HBM per device.

v0:
```python
import jax
import jax.numpy as jnp
from jax import lax
from jax.sharding import PartitionSpec as P

DP = 256
ITERS = 3


temper = 0.05


def rms_norm(values):
    return values * lax.rsqrt(jnp.mean(values * values, axis=-1, keepdims=True) + 1e-06)


def energy(zblock, unit_lists):
    scores = lax.dot_general(
        zblock, unit_lists, (((1,), (1,)), ((), ())), preferred_element_type=jnp.float32
    )
    return jnp.exp(scores / (DP * temper) - 1.0 / temper)


def update_terms(energy_blk, scale_blk, col_scale, zblock):
    weights = (scale_blk[:, None] * energy_blk * col_scale[None, :]).astype(jnp.bfloat16)
    return lax.dot_general(
        weights, zblock, (((0,), (0,)), ((), ())), preferred_element_type=jnp.float32
    )


def column_total(local_sum):
    return lax.psum(local_sum, "pts")


def on_device(tower_out, projection, centroids):
    point_rows = tower_out.shape[0]
    list_count = centroids.shape[0]
    total_points = point_rows * lax.axis_size("pts")
    total_lists = list_count * lax.axis_size("lst")
    balance = total_points / total_lists
    partial_z = jnp.dot(tower_out, projection, preferred_element_type=jnp.float32)
    summed = lax.psum(partial_z, "lst")
    normed = rms_norm(summed).astype(jnp.bfloat16)
    unit_lists = rms_norm(centroids.astype(jnp.float32)).astype(jnp.bfloat16)
    block_rows = min(512, point_rows)
    block_count = point_rows // block_rows
    blocks = normed.reshape(block_count, block_rows, DP)
    start_sums = jnp.zeros((list_count, DP), jnp.float32)
    row_scale = jnp.ones((point_rows,), jnp.float32)
    col_scale = jnp.ones((list_count,), jnp.float32)
    for sweep in range(ITERS):

        def column_step(running, inputs):
            zblock, scale_blk = inputs
            return (
                running + jnp.sum(energy(zblock, unit_lists) * scale_blk[:, None], axis=0),
                None,
            )

        column_sum = column_total(
            lax.scan(
                column_step,
                jnp.zeros((list_count,), jnp.float32),
                (blocks, row_scale.reshape(block_count, block_rows)),
            )[0]
        )
        col_scale = balance / column_sum

        def row_step(zblock, scales=col_scale):
            return jnp.sum(energy(zblock, unit_lists) * scales[None, :], axis=1)

        row_local = lax.map(row_step, blocks).reshape(point_rows)
        row_scale = 1.0 / lax.psum(row_local, "lst")

    def update_step(running, inputs):
        zblock, scale_blk = inputs
        return (
            running + update_terms(energy(zblock, unit_lists), scale_blk, col_scale, zblock),
            None,
        )

    list_sums = lax.scan(
        update_step, start_sums, (blocks, row_scale.reshape(block_count, block_rows))
    )[0]
    owned_sums = lax.psum_scatter(list_sums, "pts", scatter_dimension=0, tiled=True)
    return (rms_norm(owned_sums), jnp.log(row_scale))


def solution(mesh):
    return jax.shard_map(
        on_device,
        mesh=mesh,
        in_specs=(P("pts", "lst"), P("lst", None), P("lst", None)),
        out_specs=(P(("lst", "pts"), None), P("pts")),
        check_vma=False,
    )
```

profile of v0, /device:TPU:1, one launch (start us, length us, event | category | flops | bytes accessed | tf_op | source)
XLA Modules:
  0.0 472.1 jit_solution(6819094565466512705)
XLA Ops:
  7.2 0.0 copy-start
  7.2 0.0 copy-start.2
  7.2 0.0 all-reduce.2.cloned.1.call-start
  7.2 0.9 copy-done
  8.1 2.5 fusion.33
  10.6 0.0 all-reduce.2.cloned.1.call-update
  10.7 0.0 reduce-scatter.2.cloned.1.call-start
  10.8 0.0 copy-done.2
  10.8 0.2 fusion.30
  11.0 0.2 fusion.31
  11.2 161.0 %all-reduce.2.cloned.1.call-done = f32[2048,256]{1,0:T(8,128)} async-done(((f32[2048,256]{1,0:T(8,128)}), f32[2048,256]{1,0:T(8,128)}) %all-reduce.2.cloned.1.call-update) | async-done | bytes 2097168 | tf_op jit(solution)/shard_map/psum | solution.py:42
  172.2 0.0 copy-start.1
  172.2 2.1 multiply_reduce_fusion.5
  174.3 0.1 copy-done.1
  174.4 0.3 multiply_convert_fusion.1
  174.8 2.4 while.91
  174.8 0.6 exponential_reduce_fusion.2
  175.4 0.6 exponential_reduce_fusion.2
  176.0 0.6 exponential_reduce_fusion.2
  176.6 0.6 exponential_reduce_fusion.2
  177.2 36.4 %psum.50 = f32[1024]{0:T(1024)S(1)} all-reduce(f32[1024]{0:T(1024)S(1)} %get-tuple-element.457), channel_id=1, replica_groups=mesh['pts'=16,'lst'=16] {'pts'}, use_global_device_ids=true, to_apply=%region_6.7 | all-reduce | flops 1024 | bytes 8192 | tf_op jit(solution)/shard_map/psum | solution.py:32
  213.5 3.0 while.88
  213.6 0.7 multiply_reduce_fusion.12
  214.3 0.7 multiply_reduce_fusion.12
  215.1 0.7 multiply_reduce_fusion.12
  215.8 0.7 multiply_reduce_fusion.12
  216.6 34.3 %psum.51 = f32[2048]{0:T(1024)S(1)} all-reduce(f32[2048]{0:T(1024)S(1)} %bitcast.96), channel_id=1, replica_groups=mesh['pts'=16,'lst'=16] {'lst'}, use_global_device_ids=true, to_apply=%region_10.11 | all-reduce | flops 2048 | bytes 16384 | tf_op jit(solution)/shard_map/psum | solution.py:73
  250.9 2.7 while.92
  250.9 0.6 multiply_reduce_fusion.15
  251.6 0.6 multiply_reduce_fusion.15
  252.3 0.6 multiply_reduce_fusion.15
  253.0 0.6 multiply_reduce_fusion.15
  253.6 34.3 %psum.52 = f32[1024]{0:T(1024)S(1)} all-reduce(f32[1024]{0:T(1024)S(1)} %get-tuple-element.459), channel_id=1, replica_groups=mesh['pts'=16,'lst'=16] {'pts'}, use_global_device_ids=true, to_apply=%region_14.15 | all-reduce | flops 1024 | bytes 8192 | tf_op jit(solution)/shard_map/psum | solution.py:32
  288.0 3.0 while.89
  288.0 0.7 multiply_reduce_fusion.13
  288.7 0.7 multiply_reduce_fusion.13
  289.5 0.7 multiply_reduce_fusion.13
  290.2 0.7 multiply_reduce_fusion.13
  291.0 30.5 %psum.53 = f32[2048]{0:T(1024)S(1)} all-reduce(f32[2048]{0:T(1024)S(1)} %bitcast.97), channel_id=1, replica_groups=mesh['pts'=16,'lst'=16] {'lst'}, use_global_device_ids=true, to_apply=%region_18.19 | all-reduce | flops 2048 | bytes 16384 | tf_op jit(solution)/shard_map/psum | solution.py:73
  321.5 2.7 while.93
  321.6 0.6 multiply_reduce_fusion.16
  322.2 0.6 multiply_reduce_fusion.16
  322.9 0.6 multiply_reduce_fusion.16
  323.6 0.6 multiply_reduce_fusion.16
  324.2 33.8 %psum.54 = f32[1024]{0:T(1024)S(1)} all-reduce(f32[1024]{0:T(1024)S(1)} %get-tuple-element.461), channel_id=1, replica_groups=mesh['pts'=16,'lst'=16] {'pts'}, use_global_device_ids=true, to_apply=%region_22.23 | all-reduce | flops 1024 | bytes 8192 | tf_op jit(solution)/shard_map/psum | solution.py:32
  358.1 3.0 while.90
  358.1 0.7 multiply_reduce_fusion.14
  358.8 0.7 multiply_reduce_fusion.14
  359.6 0.7 multiply_reduce_fusion.14
  360.3 0.7 multiply_reduce_fusion.14
  361.1 33.4 %psum.55 = f32[2048]{0:T(1024)S(1)} all-reduce(f32[2048]{0:T(1024)S(1)} %bitcast.98), channel_id=1, replica_groups=mesh['pts'=16,'lst'=16] {'lst'}, use_global_device_ids=true, to_apply=%region_26.27 | all-reduce | flops 2048 | bytes 16384 | tf_op jit(solution)/shard_map/psum | solution.py:73
  394.6 0.6 fusion.32
  395.2 5.3 %while.94 = (s32[]{:T(128)}, f32[1024,256]{1,0:T(8,128)S(1)}, f32[4,512]{1,0:T(4,128)S(1)}, bf16[4,512,256]{2,1,0:T(8,128)(2,1)S(1)}, bf16[1024,256]{1,0:T(8,128...) while((s32[]{:T(128)}, f32[1024,256]{1,0:T(8,128)S(1)}, f32[4,512]{1,0:T(4,128)S(1)}, ...), condition=%wide.region_28.29_spmd.clone, body=%wide.region_27.28_spmd.clone.sunk | while | flops 540016640 | bytes 3157091 | solution.py:82
  395.2 1.3 convolution_add_fusion.2
  396.5 1.3 convolution_add_fusion.2
  397.9 1.3 convolution_add_fusion.2
  399.2 1.3 convolution_add_fusion.2
  400.5 0.0 copy-start.3
  400.5 1.0 copy-done.3
  401.5 0.0 reduce-scatter.2.cloned.1.call-update
  401.5 61.3 %reduce-scatter.2.cloned.1.call-done = f32[64,256]{1,0:T(8,128)} async-done(((f32[1024,256]{1,0:T(8,128)}), f32[64,256]{1,0:T(8,128)}) %reduce-scatter.2.cloned.1.call-update) | async-done | bytes 65552 | tf_op jit(solution)/shard_map/reduce_scatter | solution.py:85
  462.8 0.9 multiply_reduce_fusion.6
  463.7 1.6 broadcast_multiply_fusion
  (57 shorter events, 0.8 us)
Async XLA Ops:
  7.2 1.0 copy-start
  7.2 3.6 copy-start.2
  7.2 165.0 %all-reduce.2.cloned.1.call-start = ((), (), s32[]{:S(2)}) async-start(), calls=%async_computation.1 | async-start | bytes 4194304 | tf_op jit(solution)/shard_map/psum | solution.py:42
  10.7 452.1 %reduce-scatter.2.cloned.1.call-start = ((), (), s32[]{:S(2)}) async-start(), calls=%async_computation.2 | async-start | bytes 1114112 | tf_op jit(solution)/shard_map/reduce_scatter | solution.py:85
  172.2 2.2 copy-start.1
  400.5 1.0 copy-start.3
Sparse Core Ops, SparseCore 0:
  10.8 161.3 all-reduce.1
  401.7 61.0 reduce-scatter.1
where the time goes:
time: 475 us; the launch traced here: 472 us
  waiting for transfers between devices  222 us (47%)
  blocking collectives  203 us (43%)
  matrix products  23.2 us (5%)
  between operations  14.3 us (3%)
  other arithmetic  6.08 us (1%)
    psum x1, waiting for transfers between devices, on_device(): summed = lax.psum(partial_z, 'lst')  161 us
    psum x3, blocking collectives, column_total(): return lax.psum(local_sum, 'pts')  104 us
    psum x3, blocking collectives, on_device(): row_scale = 1.0 / lax.psum(row_local, 'lst')  98.2 us
    reduce_scatter x1, waiting for transfers between devices, on_device(): lax.psum_scatter(list_sums, 'pts', scatter_dimension=0, tiled=True)  61.3 us
    dot_general x24, matrix products, energy(): lax.dot_general(zblock, unit_lists, (((1,), (1,)), ((), ())), preferred_e...  15.5 us
  transfers between devices with their start and end apart: 2, of which 2 were waited for; matrix products, arithmetic and copies ran while one was open for 0% of the time, Pallas kernels for 0%

commit v1 on v0

v1 whole, which is shorter than its diff:
```python
import jax
import jax.numpy as jnp
from jax import lax
from jax.sharding import Mesh, PartitionSpec as P

DP = 256
ITERS = 3
ROWS = 128

temper = 0.05
SWAP = [(0, 1), (1, 0)]
PLANE = ("x", "yl", "c", "yh")
CHIPS = ("yh", "x", "yl")
bf16 = jnp.bfloat16
f32 = jnp.float32


def rms_norm(values):
    return values * lax.rsqrt(jnp.mean(values * values, axis=-1, keepdims=True) + 1e-06)


def energy(points, unit_lists):
    scores = lax.dot_general(
        points, unit_lists, (((1,), (1,)), ((), ())), preferred_element_type=f32
    )
    return jnp.exp(scores / (DP * temper) - 1.0 / temper)


def gather_all(values, axis, size):
    return lax.all_to_all(jnp.broadcast_to(values[None], (size,) + values.shape), axis, 0, 0)


def total(local, axis, size):
    parts = gather_all(local.reshape(-1, 128), axis, size)
    return jnp.sum(parts, axis=0).reshape(local.shape)


def on_device(tower_out, projection, centroids):
    half = lax.axis_index("yh")
    balance = 2.0
    tower = tower_out.T.reshape(64, 8, 2, ROWS)
    kept = jnp.where(half == 0, tower[:, :, 0], tower[:, :, 1]).reshape(64, 8 * ROWS)
    given = jnp.where(half == 0, tower[:, :, 1], tower[:, :, 0]).reshape(64, 8 * ROWS)
    taken = lax.ppermute(given, "yh", SWAP)
    taken_projection = lax.ppermute(projection, "yh", SWAP)
    taken_centroids = lax.ppermute(centroids, "yh", SWAP)

    contract = (((0,), (0,)), ((), ()))
    partial = lax.dot_general(kept, projection, contract, preferred_element_type=f32)
    partial += lax.dot_general(taken, taken_projection, contract, preferred_element_type=f32)
    partial = partial.astype(bf16).reshape(8, ROWS, DP)
    shares = lax.all_to_all(partial, "z", 0, 0)
    hidden = jnp.sum(shares.astype(f32), axis=0)
    own = rms_norm(hidden).astype(bf16)
    normed = gather_all(own, "z", 8).reshape(8 * ROWS, DP)

    low = jnp.where(half == 0, centroids, taken_centroids)
    high = jnp.where(half == 0, taken_centroids, centroids)
    unit_lists = rms_norm(jnp.concatenate([low, high]).astype(f32)).astype(bf16)

    row_scale = jnp.ones((8 * ROWS,), f32)
    for sweep in range(ITERS):
        column_local = jnp.sum(energy(normed, unit_lists) * row_scale[:, None], axis=0)
        col_scale = balance / total(column_local, PLANE, 32)
        row_local = jnp.sum(energy(normed, unit_lists) * col_scale[None, :], axis=1)
        row_scale = 1.0 / total(row_local, "z", 8)

    row_log = jnp.log(row_scale).reshape(8, ROWS)
    taken_log = lax.ppermute(row_log, "yh", SWAP)
    low_log = jnp.where(half == 0, row_log, taken_log)
    high_log = jnp.where(half == 0, taken_log, row_log)
    row_log = jnp.stack([low_log, high_log], axis=1).reshape(16 * ROWS)

    weights = row_scale[:, None] * energy(normed, unit_lists) * col_scale[None, :]
    list_sums = lax.dot_general(
        weights.astype(bf16), normed, (((0,), (0,)), ((), ())), preferred_element_type=f32
    )
    by_core = list_sums.reshape(16, 2, 64, DP)
    core = lax.axis_index("c")
    mine = jnp.where(core == 0, by_core[:, 0], by_core[:, 1])
    theirs = jnp.where(core == 0, by_core[:, 1], by_core[:, 0])
    mine += lax.ppermute(theirs, "c", SWAP)
    owned = jnp.sum(lax.all_to_all(mine.astype(bf16), CHIPS, 0, 0).astype(f32), axis=0)
    return (rms_norm(owned), row_log)


def solution(mesh):
    fine = Mesh(mesh.devices.reshape(4, 2, 2, 8, 2), ("x", "yl", "c", "z", "yh"))
    pts, lst = ("x", "yl", "c"), ("z", "yh")
    return jax.shard_map(
        on_device,
        mesh=fine,
        in_specs=(P(pts, lst), P(lst, None), P(lst, None)),
        out_specs=(P(lst + pts, None), P(pts)),
        check_vma=False,
    )
```

time: 475 us -> 197 us (0.41)
  waiting for transfers between devices: 222 us -> 46.6 us
  blocking collectives: 203 us -> 74.5 us
  starting transfers between devices: 0.08 us -> 24.2 us
  other arithmetic: 6.08 us -> 29.2 us
  between operations: 14.3 us -> 0.91 us
  matrix products: 23.2 us -> 10.7 us
  local copies, waits for them, and re-layouts: 2.7 us -> 9.46 us
    psum x6 -> x0, blocking collectives: 203 us -> none  [the longest x3 104 us: column_total(): return lax.psum(local_sum, 'pts')]
    psum x1 -> x0, waiting for transfers between devices: 161 us -> none  [on_device(): summed = lax.psum(partial_z, 'lst')]
    all_to_all x0 -> x6, blocking collectives: none -> 74.5 us  [gather_all(): lax.all_to_all(jnp.broadcast_to(values[None], (size,) + values.shape), ax...]
    reduce_scatter x1 -> x0, waiting for transfers between devices: 61.3 us -> none  [on_device(): lax.psum_scatter(list_sums, 'pts', scatter_dimension=0, tiled=True)]
    all_to_all x0 -> x3, waiting for transfers between devices: none -> 37 us  [the longest x1 13.6 us: gather_all(): lax.all_to_all(jnp.broadcast_to(values[None], (size,) + values.shape), ax...]
    reduce_sum x0 -> x13, other arithmetic: none -> 20.4 us  [the longest x3 12.1 us: on_device(): row_local = jnp.sum(energy(normed, unit_lists) * col_scale[None, :], axis=1)]
    all_to_all x0 -> x3, starting transfers between devices: none -> 14.6 us  [the longest x1 7.54 us: on_device(): shares = lax.all_to_all(partial, 'z', 0, 0)]
    dot_general x29 -> x4, matrix products: 23.2 us -> 10.7 us  [the longest x1 5.01 us: energy(): lax.dot_general(points, unit_lists, (((1,), (1,)), ((), ())), preferred_e...]
  transfers between devices with their start and end apart: 2 -> 8, of which waited for: 2 -> 6; matrix products, arithmetic and copies ran while one was open for 0% -> 2% of each run, Pallas kernels for 0% -> 0%
where the time goes in v1:
time: 197 us; the launch traced here: 196 us
  blocking collectives  74.5 us (38%)
  waiting for transfers between devices  46.6 us (24%)
  other arithmetic  29.2 us (15%)
  starting transfers between devices  24.2 us (12%)
  matrix products  10.7 us (5%)
  local copies, waits for them, and re-layouts  9.46 us (5%)
    all_to_all x6, blocking collectives, gather_all(): lax.all_to_all(jnp.broadcast_to(values[None], (size,) + values.shape), ax...  74.5 us
    all_to_all x1, waiting for transfers between devices, gather_all(): lax.all_to_all(jnp.broadcast_to(values[None], (size,) + values.shape), ax...  13.6 us
    all_to_all x1, waiting for transfers between devices, on_device(): shares = lax.all_to_all(partial, 'z', 0, 0)  13 us
    reduce_sum x3, other arithmetic, on_device(): row_local = jnp.sum(energy(normed, unit_lists) * col_scale[None, :], axis=1)  12.1 us
    all_to_all x1, waiting for transfers between devices, on_device(): lax.all_to_all(mine.astype(bf16), CHIPS, 0, 0).astype(f32)  10.4 us
    reduce_sum x2, other arithmetic, on_device(): jnp.sum(energy(normed, unit_lists) * row_scale[:, None], axis=0)  8.01 us
    all_to_all x1, starting transfers between devices, on_device(): shares = lax.all_to_all(partial, 'z', 0, 0)  7.54 us
    convert_element_type x1, local copies, waits for them, and re-layouts, on_device(): weights.astype(bf16)  6.4 us
  transfers between devices with their start and end apart: 8, of which 6 were waited for; matrix products, arithmetic and copies ran while one was open for 2% of the time, Pallas kernels for 0%

profile of v1, /device:TPU:1, one launch (start us, length us, event | category | flops | bytes accessed | tf_op | source)
XLA Modules:
  0.0 195.6 jit_solution(4616620908559193964)
XLA Ops:
  0.6 0.0 copy-start
  0.6 1.2 reshape.127
  1.8 0.4 fusion.15
  2.3 3.8 %collective-permute-start = (bf16[64,1024]{1,0:T(8,128)(2,1)S(1)}, bf16[64,1024]{1,0:T(8,128)(2,1)S(1)}, u32[]{:S(2)}, u32[]{:S(2)}) collective-permute-start(bf16[64,1024]{1,0:T(8,128)(2,1)S(1)} %bitcast.79), channel_id=1, source_target_pairs={{0,1},{1,0},{2,3},{3,2},{4,5},{5,4},{6,7},{7,6},{8,9},{9,8},{10,11... | collective-permute-start | bytes 393224 | tf_op jit(solution)/shard_map/ppermute | solution.py:44
  6.1 0.1 collective-permute-start.1
  6.2 1.1 fusion.9
  7.3 3.9 %collective-permute-done.1 = bf16[64,256]{1,0:T(8,128)(2,1)S(1)} collective-permute-done((bf16[64,256]{1,0:T(8,128)(2,1)}, bf16[64,256]{1,0:T(8,128)(2,1)S(1)}, u32[]{:S(2)}, u32[]{:S(2)}) %collective-permute-start.1) | collective-permute-done | bytes 32800 | tf_op jit(solution)/shard_map/ppermute | solution.py:45
  11.2 0.0 collective-permute-done
  11.2 1.1 fusion.3
  12.4 7.5 %all-to-all-start = ((bf16[8,128,256]{2,1,0:T(8,128)(2,1)}), bf16[8,128,256]{2,1,0:T(8,128)(2,1)S(1)}, u32[]{:S(2)}, u32[]{:S(2)}) async-start(bf16[8,128,256]{2,1,0:T(8,128)(2,1)} %bitcast.1), calls=%async_computation | async-start | bytes 1048576 | tf_op jit(solution)/shard_map/all_to_all | solution.py:52
  19.9 2.1 %collective-permute-start.2 = (bf16[1024,256]{1,0:T(8,128)(2,1)}, bf16[1024,256]{1,0:T(8,128)(2,1)S(1)}, u32[]{:S(2)}, u32[]{:S(2)}) collective-permute-start(bf16[1024,256]{1,0:T(8,128)(2,1)} %param.5), channel_id=1, source_target_pairs={{0,1},{1,0},{2,3},{3,2},{4,5},{5,4},{6,7},{7,6},{8,9},{9,8},{10,11... | collective-permute-start | bytes 1572872 | tf_op jit(solution)/shard_map/ppermute | solution.py:46
  22.0 13.0 %all-to-all-done = bf16[8,128,256]{2,1,0:T(8,128)(2,1)S(1)} async-done(((bf16[8,128,256]{2,1,0:T(8,128)(2,1)}), bf16[8,128,256]{2,1,0:T(8,128)(2,1)S(1)}, u32[]{:S(2)}, u32[]{:S(2)}) %all-to-all-start) | async-done | bytes 524320 | tf_op jit(solution)/shard_map/all_to_all | solution.py:52
  35.0 0.1 convert_reduce_fusion.1
  35.1 0.1 multiply_reduce_fusion.5
  35.2 0.1 multiply_convert_fusion.1
  35.3 0.8 broadcast_in_dim.26
  36.1 3.5 %all-to-all-start.1 = ((bf16[8,128,256]{2,1,0:T(8,128)(2,1)}), bf16[8,128,256]{2,1,0:T(8,128)(2,1)S(1)}, u32[]{:S(2)}, u32[]{:S(2)}) async-start(bf16[8,128,256]{2,1,0:T(8,128)(2,1)} %broadcast_in_dim.26), calls=%async_computation.1 | async-start | bytes 1048576 | tf_op jit(solution)/shard_map/all_to_all | solution.py:30
  39.6 0.0 collective-permute-done.2
  39.6 0.0 copy-done
  39.6 0.1 broadcast_select_fusion.1
  39.7 0.3 fusion.1
  40.1 13.6 %all-to-all-done.1 = bf16[8,128,256]{2,1,0:T(8,128)(2,1)S(1)} async-done(((bf16[8,128,256]{2,1,0:T(8,128)(2,1)}), bf16[8,128,256]{2,1,0:T(8,128)(2,1)S(1)}, u32[]{:S(2)}, u32[]{:S(2)}) %all-to-all-start.1) | async-done | bytes 524320 | tf_op jit(solution)/shard_map/all_to_all | solution.py:30
  53.7 5.0 %fusion.16 = (f32[2048]{0:T(1024)S(1)}, f32[1024,2048]{1,0:T(8,128)}) fusion(bf16[1024,256]{1,0:T(8,128)(2,1)S(1)} %bitcast.74, f32[2048]{0:T(1024)S(1)} %add_rsqrt_fusion, bf16[1024,256]{1,0:T(8,128)(2,1)S(1)} %get-tuple-element.3, bf16[1024,256]{1,0:T(8,128)(2,1)S(1)} %get-tuple-element.2), kind=kOutput, calls=%fused_computation.51 | convolution fusion | flops 1083176960 | bytes 9977856 | tf_op jit(solution)/shard_map/dot_general | solution.py:23
  58.7 20.0 %all_to_all.45 = f32[32,16,128]{2,1,0:T(8,128)S(1)} all-to-all(f32[32,16,128]{2,1,0:T(8,128)S(1)} %broadcast_in_dim.28), channel_id=1, replica_groups=mesh['x'=4,'yl'=2,'c'=2,'z'=8,'yh'=2] {'x','yl','c','yh'}, dimensions={0} | all-to-all | bytes 524288 | tf_op jit(solution)/shard_map/all_to_all | solution.py:30
  78.8 4.0 %multiply_reduce_fusion.4 = f32[1024]{0:T(1024)S(1)} fusion(f32[1024,2048]{1,0:T(8,128)} %get-tuple-element.12, f32[2048]{0:T(1024)S(1)} %divide_bitcast_fusion.2), kind=kLoop, calls=%fused_computation.5 | loop fusion | flops 4193280 | bytes 8400896 | tf_op jit(solution)/shard_map/reduce_sum | solution.py:65
  82.8 9.2 %all_to_all.46 = f32[8,8,128]{2,1,0:T(8,128)S(1)} all-to-all(f32[8,8,128]{2,1,0:T(8,128)S(1)} %broadcast_in_dim.30), channel_id=1, replica_groups=mesh['x'=4,'yl'=2,'c'=2,'z'=8,'yh'=2] {'z'}, dimensions={0} | all-to-all | bytes 65536 | tf_op jit(solution)/shard_map/all_to_all | solution.py:30
  92.1 4.0 %multiply_reduce_fusion.3 = f32[2048]{0:T(1024)S(1)} fusion(f32[1024,2048]{1,0:T(8,128)} %get-tuple-element.12, f32[1024]{0:T(1024)S(1)} %divide_bitcast_fusion.4), kind=kLoop, calls=%fused_computation.4 | loop fusion | flops 4192256 | bytes 8400896 | tf_op jit(solution)/shard_map/reduce_sum | solution.py:63
  96.2 13.4 %all_to_all.47 = f32[32,16,128]{2,1,0:T(8,128)S(1)} all-to-all(f32[32,16,128]{2,1,0:T(8,128)S(1)} %broadcast_in_dim.64), channel_id=1, replica_groups=mesh['x'=4,'yl'=2,'c'=2,'z'=8,'yh'=2] {'x','yl','c','yh'}, dimensions={0} | all-to-all | bytes 524288 | tf_op jit(solution)/shard_map/all_to_all | solution.py:30
  109.6 4.0 %multiply_reduce_fusion.2 = f32[1024]{0:T(1024)S(1)} fusion(f32[1024,2048]{1,0:T(8,128)} %get-tuple-element.12, f32[2048]{0:T(1024)S(1)} %divide_bitcast_fusion.1), kind=kLoop, calls=%fused_computation.3 | loop fusion | flops 4193280 | bytes 8400896 | tf_op jit(solution)/shard_map/reduce_sum | solution.py:65
  113.6 9.2 %all_to_all.48 = f32[8,8,128]{2,1,0:T(8,128)S(1)} all-to-all(f32[8,8,128]{2,1,0:T(8,128)S(1)} %broadcast_in_dim.66), channel_id=1, replica_groups=mesh['x'=4,'yl'=2,'c'=2,'z'=8,'yh'=2] {'z'}, dimensions={0} | all-to-all | bytes 65536 | tf_op jit(solution)/shard_map/all_to_all | solution.py:30
  122.9 4.0 %multiply_reduce_fusion.1 = f32[2048]{0:T(1024)S(1)} fusion(f32[1024,2048]{1,0:T(8,128)} %get-tuple-element.12, f32[1024]{0:T(1024)S(1)} %divide_bitcast_fusion.3), kind=kLoop, calls=%fused_computation.2 | loop fusion | flops 4192256 | bytes 8400896 | tf_op jit(solution)/shard_map/reduce_sum | solution.py:63
  126.9 13.4 %all_to_all.49 = f32[32,16,128]{2,1,0:T(8,128)S(1)} all-to-all(f32[32,16,128]{2,1,0:T(8,128)S(1)} %broadcast_in_dim.68), channel_id=1, replica_groups=mesh['x'=4,'yl'=2,'c'=2,'z'=8,'yh'=2] {'x','yl','c','yh'}, dimensions={0} | all-to-all | bytes 524288 | tf_op jit(solution)/shard_map/all_to_all | solution.py:30
  140.4 4.0 %multiply_reduce_fusion = f32[1024]{0:T(1024)S(1)} fusion(f32[1024,2048]{1,0:T(8,128)} %get-tuple-element.12, f32[2048]{0:T(1024)S(1)} %divide_bitcast_fusion), kind=kLoop, calls=%fused_computation.1 | loop fusion | flops 4193280 | bytes 8400896 | tf_op jit(solution)/shard_map/reduce_sum | solution.py:65
  144.4 9.2 %all_to_all.50 = f32[8,8,128]{2,1,0:T(8,128)S(1)} all-to-all(f32[8,8,128]{2,1,0:T(8,128)S(1)} %broadcast_in_dim.70), channel_id=1, replica_groups=mesh['x'=4,'yl'=2,'c'=2,'z'=8,'yh'=2] {'z'}, dimensions={0} | all-to-all | bytes 65536 | tf_op jit(solution)/shard_map/all_to_all | solution.py:30
  153.7 0.8 collective-permute-start.4
  154.4 3.4 %collective-permute-done.4 = f32[8,128]{1,0:T(8,128)S(1)} collective-permute-done((f32[8,128]{1,0:T(8,128)S(1)}, f32[8,128]{1,0:T(8,128)S(1)}, u32[]{:S(2)}, u32[]{:S(2)}) %collective-permute-start.4) | collective-permute-done | bytes 4128 | tf_op jit(solution)/shard_map/ppermute | solution.py:69
  157.9 6.1 %fusion = bf16[2048,1024]{0,1:T(8,128)(2,1)} fusion(f32[1024,2048]{1,0:T(8,128)} %get-tuple-element.12, f32[1024]{0:T(1024)S(1)} %get-tuple-element.10, f32[2048]{0:T(1024)S(1)} %divide_bitcast_fusion), kind=kLoop, calls=%fused_computation.7 | loop fusion | flops 6291456 | bytes 12595200 | tf_op jit(solution)/shard_map/convert_element_type | solution.py:76
  164.0 6.4 %copy.20 = bf16[2048,1024]{1,0:T(8,128)(2,1)} copy(bf16[2048,1024]{0,1:T(8,128)(2,1)} %fusion) | data formatting | bytes 8388608 | tf_op jit(solution)/shard_map/convert_element_type | solution.py:76
  170.4 3.5 %fusion.17 = f32[16,2,64,256]{3,2,1,0:T(8,128)S(1)} fusion(bf16[16,2,64,1024]{3,2,1,0:T(8,128)(2,1)} %bitcast.73, bf16[1024,256,1,1]{1,0,3,2:T(8,128)(2,1)S(1)} %bitcast.75), kind=kOutput, calls=%fused_computation.52 | convolution fusion | flops 1073741824 | bytes 6815744 | tf_op jit(solution)/shard_map/dot_general | solution.py:75
  173.9 0.1 select_bitcast_fusion
  174.0 2.8 %collective-permute-start.3 = (f32[16,64,256]{2,1,0:T(8,128)S(1)}, f32[16,64,256]{2,1,0:T(8,128)S(1)}, u32[]{:S(2)}, u32[]{:S(2)}) collective-permute-start(f32[16,64,256]{2,1,0:T(8,128)S(1)} %select_bitcast_fusion), channel_id=1, source_target_pairs={{0,16},{16,0},{1,17},{17,1},{2,18},{18,2},{3,19},{19,3},{4,20},{20... | collective-permute-start | bytes 3145736 | tf_op jit(solution)/shard_map/ppermute | solution.py:82
  176.8 2.3 %collective-permute-done.3 = f32[16,64,256]{2,1,0:T(8,128)S(1)} collective-permute-done((f32[16,64,256]{2,1,0:T(8,128)S(1)}, f32[16,64,256]{2,1,0:T(8,128)S(1)}, u32[]{:S(2)}, u32[]{:S(2)}) %collective-permute-start.3) | collective-permute-done | bytes 1048608 | tf_op jit(solution)/shard_map/ppermute | solution.py:82
  179.1 1.0 fusion.7
  180.1 3.6 %all-to-all-start.8 = ((bf16[16,64,256]{2,1,0:T(8,128)(2,1)}), bf16[16,64,256]{2,1,0:T(8,128)(2,1)S(1)}, u32[]{:S(2)}, u32[]{:S(2)}) async-start(bf16[16,64,256]{2,1,0:T(8,128)(2,1)} %fusion.7), calls=%async_computation.8 | async-start | bytes 1048576 | tf_op jit(solution)/shard_map/all_to_all | solution.py:83
  183.7 0.6 copy.25
  184.3 10.4 %all-to-all-done.8 = bf16[16,64,256]{2,1,0:T(8,128)(2,1)S(1)} async-done(((bf16[16,64,256]{2,1,0:T(8,128)(2,1)}), bf16[16,64,256]{2,1,0:T(8,128)(2,1)S(1)}, u32[]{:S(2)}, u32[]{:S(2)}) %all-to-all-start.8) | async-done | bytes 524320 | tf_op jit(solution)/shard_map/all_to_all | solution.py:83
  194.7 0.1 convert_reduce_fusion
  194.8 0.1 multiply_reduce_fusion.6
  194.9 0.7 broadcast_multiply_fusion
  (25 shorter events, 0.3 us)
Async XLA Ops:
  0.6 39.0 %copy-start = (bf16[1024,256]{1,0:T(8,128)(2,1)S(1)}, bf16[1024,256]{1,0:T(8,128)(2,1)}, u32[]{:S(2)}) copy-start(bf16[1024,256]{1,0:T(8,128)(2,1)} %param.5) | copy-start | bytes 1572868
  2.3 9.0 %collective-permute-start = (bf16[64,1024]{1,0:T(8,128)(2,1)S(1)}, bf16[64,1024]{1,0:T(8,128)(2,1)S(1)}, u32[]{:S(2)}, u32[]{:S(2)}) collective-permute-start(bf16[64,1024]{1,0:T(8,128)(2,1)S(1)} %bitcast.79), channel_id=1, source_target_pairs={{0,1},{1,0},{2,3},{3,2},{4,5},{5,4},{6,7},{7,6},{8,9},{9,8},{10,11... | collective-permute-start | bytes 393224 | tf_op jit(solution)/shard_map/ppermute | solution.py:44
  6.1 5.1 %collective-permute-start.1 = (bf16[64,256]{1,0:T(8,128)(2,1)}, bf16[64,256]{1,0:T(8,128)(2,1)S(1)}, u32[]{:S(2)}, u32[]{:S(2)}) collective-permute-start(bf16[64,256]{1,0:T(8,128)(2,1)} %param.4), channel_id=1, source_target_pairs={{0,1},{1,0},{2,3},{3,2},{4,5},{5,4},{6,7},{7,6},{8,9},{9,8},{10,11... | collective-permute-start | bytes 98312 | tf_op jit(solution)/shard_map/ppermute | solution.py:45
  12.4 22.6 %all-to-all-start = ((bf16[8,128,256]{2,1,0:T(8,128)(2,1)}), bf16[8,128,256]{2,1,0:T(8,128)(2,1)S(1)}, u32[]{:S(2)}, u32[]{:S(2)}) async-start(bf16[8,128,256]{2,1,0:T(8,128)(2,1)} %bitcast.1), calls=%async_computation | async-start | bytes 1048576 | tf_op jit(solution)/shard_map/all_to_all | solution.py:52
  19.9 19.7 %collective-permute-start.2 = (bf16[1024,256]{1,0:T(8,128)(2,1)}, bf16[1024,256]{1,0:T(8,128)(2,1)S(1)}, u32[]{:S(2)}, u32[]{:S(2)}) collective-permute-start(bf16[1024,256]{1,0:T(8,128)(2,1)} %param.5), channel_id=1, source_target_pairs={{0,1},{1,0},{2,3},{3,2},{4,5},{5,4},{6,7},{7,6},{8,9},{9,8},{10,11... | collective-permute-start | bytes 1572872 | tf_op jit(solution)/shard_map/ppermute | solution.py:46
  36.1 17.6 %all-to-all-start.1 = ((bf16[8,128,256]{2,1,0:T(8,128)(2,1)}), bf16[8,128,256]{2,1,0:T(8,128)(2,1)S(1)}, u32[]{:S(2)}, u32[]{:S(2)}) async-start(bf16[8,128,256]{2,1,0:T(8,128)(2,1)} %broadcast_in_dim.26), calls=%async_computation.1 | async-start | bytes 1048576 | tf_op jit(solution)/shard_map/all_to_all | solution.py:30
  153.7 4.2 %collective-permute-start.4 = (f32[8,128]{1,0:T(8,128)S(1)}, f32[8,128]{1,0:T(8,128)S(1)}, u32[]{:S(2)}, u32[]{:S(2)}) collective-permute-start(f32[8,128]{1,0:T(8,128)S(1)} %fusion.12), channel_id=1, source_target_pairs={{0,1},{1,0},{2,3},{3,2},{4,5},{5,4},{6,7},{7,6},{8,9},{9,8},{10,11... | collective-permute-start | bytes 12296 | tf_op jit(solution)/shard_map/ppermute | solution.py:69
  174.0 5.1 %collective-permute-start.3 = (f32[16,64,256]{2,1,0:T(8,128)S(1)}, f32[16,64,256]{2,1,0:T(8,128)S(1)}, u32[]{:S(2)}, u32[]{:S(2)}) collective-permute-start(f32[16,64,256]{2,1,0:T(8,128)S(1)} %select_bitcast_fusion), channel_id=1, source_target_pairs={{0,16},{16,0},{1,17},{17,1},{2,18},{18,2},{3,19},{19,3},{4,20},{20... | collective-permute-start | bytes 3145736 | tf_op jit(solution)/shard_map/ppermute | solution.py:82
  180.1 14.6 %all-to-all-start.8 = ((bf16[16,64,256]{2,1,0:T(8,128)(2,1)}), bf16[16,64,256]{2,1,0:T(8,128)(2,1)S(1)}, u32[]{:S(2)}, u32[]{:S(2)}) async-start(bf16[16,64,256]{2,1,0:T(8,128)(2,1)} %fusion.7), calls=%async_computation.8 | async-start | bytes 1048576 | tf_op jit(solution)/shard_map/all_to_all | solution.py:83

commit v2 on v1

v2 whole, which is shorter than its diff:
```python
import jax
import jax.numpy as jnp
from jax import lax
from jax.experimental import pallas as pl
from jax.experimental.pallas import tpu as pltpu
from jax.sharding import Mesh, PartitionSpec as P

DP = 256
ITERS = 3
ROWS = 128

temper = 0.05
SWAP = [(0, 1), (1, 0)]
PLANE = ("x", "yl", "c", "yh")
CHIPS = ("yh", "x", "yl")
bf16 = jnp.bfloat16
f32 = jnp.float32


def rms_norm(values):
    return values * lax.rsqrt(jnp.mean(values * values, axis=-1, keepdims=True) + 1e-06)


VMEM = pltpu.VMEM
LIMIT = pltpu.CompilerParams(vmem_limit_bytes=40 * 2**20)


def whole(count):
    return [pl.BlockSpec(memory_space=VMEM)] * count


def stay(array):
    return pltpu.with_memory_space_constraint(array, VMEM)


def split_rows(row):
    high = row.astype(bf16).astype(f32)
    index = lax.broadcasted_iota(jnp.int32, (16, row.shape[1]), 0)
    lhs = jnp.where(index == 0, high, jnp.where(index == 1, row - high, 0.0))
    return lhs.astype(bf16)


def to_lanes(tile):
    return jnp.concatenate([tile[k : k + 1] for k in range(tile.shape[0])], axis=1)


def to_tile(rows):
    line = rows[0:1] + rows[1:2]
    return jnp.concatenate(
        [line[:, 128 * k : 128 * (k + 1)] for k in range(line.shape[1] // 128)], axis=0
    )


def add_parts(ref):
    tile = ref[0]
    for k in range(1, ref.shape[0]):
        tile += ref[k]
    return tile


def column_sums(row_scale, energy_t):
    return to_tile(
        lax.dot_general(
            split_rows(to_lanes(row_scale)),
            energy_t,
            (((1,), (1,)), ((), ())),
            preferred_element_type=f32,
        )
    )


def energy_kernel(points_ref, lists_ref, energy_ref, column_ref):
    points = points_ref[...].reshape(8 * ROWS, DP)
    for k in range(8):
        rows = pl.ds(256 * k, 256)
        scores = lax.dot_general(
            lists_ref[rows, :], points, (((1,), (1,)), ((), ())), preferred_element_type=f32
        )
        energy_ref[rows, :] = jnp.exp(scores * (1.0 / (DP * temper)) - 1.0 / temper).astype(bf16)
    local = column_sums(jnp.ones((8, 128), f32), energy_ref[...])
    column_ref[...] = jnp.broadcast_to(local[None], column_ref.shape)


def row_kernel(parts_ref, energy_ref, row_ref):
    col_scale = 2.0 / add_parts(parts_ref)
    local = to_tile(
        jnp.dot(split_rows(to_lanes(col_scale)), energy_ref[...], preferred_element_type=f32)
    )
    row_ref[...] = jnp.broadcast_to(local[None], row_ref.shape)


def column_kernel(parts_ref, energy_ref, column_ref):
    local = column_sums(1.0 / add_parts(parts_ref), energy_ref[...])
    column_ref[...] = jnp.broadcast_to(local[None], column_ref.shape)


def down_lanes(row):
    return jnp.transpose(jnp.broadcast_to(row, (128, 128)))


def update_kernel(core_ref, rows_ref, columns_ref, energy_ref, points_ref, mine_ref, other_ref):
    core = core_ref[0]
    row_scale = 1.0 / add_parts(rows_ref)
    col_scale = 2.0 / add_parts(columns_ref)
    scaled = []
    for k in range(8):
        factor = down_lanes(row_scale[k : k + 1])
        block = points_ref[k].astype(f32)
        scaled.append((block * jnp.concatenate([factor, factor], axis=1)).astype(bf16))
    scaled = jnp.concatenate(scaled, axis=0)
    for k in range(16):
        factor = down_lanes(col_scale[k : k + 1])
        sums = jnp.dot(
            energy_ref[pl.ds(128 * k, 128), :], scaled, preferred_element_type=f32
        ) * jnp.concatenate([factor, factor], axis=1)
        mine_ref[k] = jnp.where(core == 0, sums[:64], sums[64:])
        other_ref[k] = jnp.where(core == 0, sums[64:], sums[:64])


def parts_shape(count, rows):
    return jax.ShapeDtypeStruct((count, rows, 128), f32)


def gather_all(values, axis, size):
    return lax.all_to_all(jnp.broadcast_to(values[None], (size,) + values.shape), axis, 0, 0)


def on_device(tower_out, projection, centroids):
    half = lax.axis_index("yh")
    tower = tower_out.T.reshape(64, 8, 2, ROWS)
    kept = jnp.where(half == 0, tower[:, :, 0], tower[:, :, 1]).reshape(64, 8 * ROWS)
    given = jnp.where(half == 0, tower[:, :, 1], tower[:, :, 0]).reshape(64, 8 * ROWS)
    taken = lax.ppermute(given, "yh", SWAP)
    taken_projection = lax.ppermute(projection, "yh", SWAP)
    taken_centroids = lax.ppermute(centroids, "yh", SWAP)

    contract = (((0,), (0,)), ((), ()))
    partial = lax.dot_general(kept, projection, contract, preferred_element_type=f32)
    partial += lax.dot_general(taken, taken_projection, contract, preferred_element_type=f32)
    partial = partial.astype(bf16).reshape(8, ROWS, DP)
    shares = lax.all_to_all(partial, "z", 0, 0)
    hidden = jnp.sum(shares.astype(f32), axis=0)
    own = rms_norm(hidden).astype(bf16)
    points = gather_all(own, "z", 8)

    low = jnp.where(half == 0, centroids, taken_centroids)
    high = jnp.where(half == 0, taken_centroids, centroids)
    unit_lists = rms_norm(jnp.concatenate([low, high]).astype(f32)).astype(bf16)

    energy, columns = pl.pallas_call(
        energy_kernel,
        out_shape=(VMEM((2048, 1024), bf16), parts_shape(32, 16)),
        in_specs=whole(2),
        out_specs=whole(2),
        compiler_params=LIMIT,
        name="energy",
    )(points, unit_lists)
    for sweep in range(ITERS):
        columns = lax.all_to_all(columns, PLANE, 0, 0)
        rows = pl.pallas_call(
            row_kernel,
            out_shape=parts_shape(8, 8),
            in_specs=whole(2),
            out_specs=whole(1)[0],
            compiler_params=LIMIT,
            name="row_sums",
        )(columns, stay(energy))
        rows = lax.all_to_all(rows, "z", 0, 0)
        if sweep < ITERS - 1:
            columns = pl.pallas_call(
                column_kernel,
                out_shape=parts_shape(32, 16),
                in_specs=whole(2),
                out_specs=whole(1)[0],
                compiler_params=LIMIT,
                name="column_sums",
            )(rows, stay(energy))

    row_log = jnp.log(1.0 / jnp.sum(rows, axis=0))
    taken_log = lax.ppermute(row_log, "yh", SWAP)
    mine, other = pl.pallas_call(
        update_kernel,
        out_shape=(jax.ShapeDtypeStruct((16, 64, DP), f32),) * 2,
        in_specs=[pl.BlockSpec(memory_space=pltpu.SMEM)] + whole(4),
        out_specs=whole(2),
        compiler_params=LIMIT,
        name="update",
    )(lax.axis_index("c").reshape(1), rows, columns, stay(energy), points)
    mine += lax.ppermute(other, "c", SWAP)
    owned = jnp.sum(lax.all_to_all(mine.astype(bf16), CHIPS, 0, 0).astype(f32), axis=0)

    low_log = jnp.where(half == 0, row_log, taken_log)
    high_log = jnp.where(half == 0, taken_log, row_log)
    row_log = jnp.stack([low_log, high_log], axis=1).reshape(16 * ROWS)
    return (rms_norm(owned), row_log)


def solution(mesh):
    fine = Mesh(mesh.devices.reshape(4, 2, 2, 8, 2), ("x", "yl", "c", "z", "yh"))
    pts, lst = ("x", "yl", "c"), ("z", "yh")
    return jax.shard_map(
        on_device,
        mesh=fine,
        in_specs=(P(pts, lst), P(lst, None), P(lst, None)),
        out_specs=(P(lst + pts, None), P(pts)),
        check_vma=False,
    )
```

time: 197 us -> 162 us (0.82)
  other arithmetic: 29.2 us -> 4.78 us
  blocking collectives: 74.5 us -> 63.2 us
  matrix products: 10.7 us -> 1.45 us
  Pallas kernels: 0 us -> 9.17 us
  local copies, waits for them, and re-layouts: 9.46 us -> 4.52 us
  starting transfers between devices: 24.2 us -> 27.4 us
  waiting for transfers between devices: 46.6 us -> 49.7 us
    reduce_sum x11 -> x1, other arithmetic: 20.2 us -> 0.01 us  [on_device(): row_log = jnp.log(1.0 / jnp.sum(rows, axis=0))]
    all_to_all x6 -> x5, blocking collectives: 74.5 us -> 63.2 us  [the longest x3 44.7 us: on_device(): columns = lax.all_to_all(columns, PLANE, 0, 0)]
    pallas_call x0 -> x7, Pallas kernels: none -> 9.17 us  [the longest x1 2.68 us: on_device(): pl.pallas_call(energy_kernel, out_shape=(VMEM((2048, 1024), bf16), parts_...]
    dot_general x2 -> x0, matrix products: 8.47 us -> none  [the longest x1 5.01 us: energy(): lax.dot_general(points, unit_lists, (((1,), (1,)), ((), ())), preferred_e...]
    all_to_all x0 -> x1, waiting for transfers between devices: none -> 6.6 us  [on_device(): rows = lax.all_to_all(rows, 'z', 0, 0)]
    convert_element_type x1 -> x0, local copies, waits for them, and re-layouts: 6.4 us -> none  [on_device(): weights.astype(bf16)]
    convert_element_type x1, other arithmetic: 6.11 us -> 0.34 us  [on_device(): unit_lists = rms_norm(jnp.concatenate([low, high]).astype(f32)).astype(bf16)]
    ppermute x1, waiting for transfers between devices: 0.01 us -> 4.95 us  [on_device(): taken = lax.ppermute(given, 'yh', SWAP)]
  transfers between devices with their start and end apart: 8 -> 9, of which waited for: 6 -> 7; matrix products, arithmetic and copies ran while one was open for 2% -> 3% of each run, Pallas kernels for 0% -> 0%
where the time goes in v2:
time: 162 us; the launch traced here: 161 us
  blocking collectives  63.2 us (39%)
  waiting for transfers between devices  49.7 us (31%)
  starting transfers between devices  27.4 us (17%)
  Pallas kernels  9.17 us (6%)
  other arithmetic  4.78 us (3%)
  local copies, waits for them, and re-layouts  4.52 us (3%)
    all_to_all x3, blocking collectives, on_device(): columns = lax.all_to_all(columns, PLANE, 0, 0)  44.7 us
    all_to_all x2, blocking collectives, on_device(): rows = lax.all_to_all(rows, 'z', 0, 0)  18.5 us
    all_to_all x1, waiting for transfers between devices, on_device(): shares = lax.all_to_all(partial, 'z', 0, 0)  15 us
    all_to_all x1, waiting for transfers between devices, gather_all(): lax.all_to_all(jnp.broadcast_to(values[None], (size,) + values.shape), ax...  13.3 us
    all_to_all x1, starting transfers between devices, on_device(): shares = lax.all_to_all(partial, 'z', 0, 0)  8.19 us
    all_to_all x1, waiting for transfers between devices, on_device(): rows = lax.all_to_all(rows, 'z', 0, 0)  6.6 us
    all_to_all x1, waiting for transfers between devices, on_device(): lax.all_to_all(mine.astype(bf16), CHIPS, 0, 0).astype(f32)  5.65 us
    ppermute x1, waiting for transfers between devices, on_device(): taken = lax.ppermute(given, 'yh', SWAP)  4.95 us
  transfers between devices with their start and end apart: 9, of which 7 were waited for; matrix products, arithmetic and copies ran while one was open for 3% of the time, Pallas kernels for 0%

profile of v2, /device:TPU:1, one launch (start us, length us, event | category | flops | bytes accessed | tf_op | source)
XLA Modules:
  0.0 161.0 jit_solution(6687031049158527553)
XLA Ops:
  0.6 0.0 copy-start.3
  0.6 3.8 %collective-permute-start.1 = (bf16[64,256]{1,0:T(8,128)(2,1)}, bf16[64,256]{1,0:T(8,128)(2,1)S(1)}, u32[]{:S(2)}, u32[]{:S(2)}) collective-permute-start(bf16[64,256]{1,0:T(8,128)(2,1)} %param.4), channel_id=1, source_target_pairs={{0,1},{1,0},{2,3},{3,2},{4,5},{5,4},{6,7},{7,6},{8,9},{9,8},{10,11... | collective-permute-start | bytes 98312 | tf_op jit(solution)/shard_map/ppermute | solution.py:134
  4.5 1.1 reshape.67
  5.6 0.4 fusion.6
  6.0 0.0 copy-start.2
  6.1 0.1 collective-permute-start
  6.2 0.0 copy-done.3
  6.2 0.3 fusion.3
  6.5 0.0 collective-permute-done.1
  6.5 5.0 %collective-permute-done = bf16[64,1024]{1,0:T(8,128)(2,1)S(1)} collective-permute-done((bf16[64,1024]{1,0:T(8,128)(2,1)S(1)}, bf16[64,1024]{1,0:T(8,128)(2,1)S(1)}, u32[]{:S(2)}, u32[]{:S(2)}) %collective-permute-start) | collective-permute-done | bytes 131104 | tf_op jit(solution)/shard_map/ppermute | solution.py:133
  11.5 1.1 fusion.2
  12.6 8.2 %all-to-all-start = ((bf16[8,128,256]{2,1,0:T(8,128)(2,1)}), bf16[8,128,256]{2,1,0:T(8,128)(2,1)S(1)}, u32[]{:S(2)}, u32[]{:S(2)}) async-start(bf16[8,128,256]{2,1,0:T(8,128)(2,1)} %bitcast.2), calls=%async_computation | async-start | bytes 1048576 | tf_op jit(solution)/shard_map/all_to_all | solution.py:141
  20.8 0.0 copy-done.2
  20.8 0.1 collective-permute-start.2
  20.9 15.0 %all-to-all-done = bf16[8,128,256]{2,1,0:T(8,128)(2,1)S(1)} async-done(((bf16[8,128,256]{2,1,0:T(8,128)(2,1)}), bf16[8,128,256]{2,1,0:T(8,128)(2,1)S(1)}, u32[]{:S(2)}, u32[]{:S(2)}) %all-to-all-start) | async-done | bytes 524320 | tf_op jit(solution)/shard_map/all_to_all | solution.py:141
  35.9 0.1 convert_reduce_fusion.1
  35.9 0.1 multiply_reduce_fusion
  36.1 0.1 multiply_convert_fusion
  36.2 0.8 broadcast_in_dim.2
  37.0 3.5 %all-to-all-start.1 = ((bf16[8,128,256]{2,1,0:T(8,128)(2,1)}), bf16[8,128,256]{2,1,0:T(8,128)(2,1)S(1)}, u32[]{:S(2)}, u32[]{:S(2)}) async-start(bf16[8,128,256]{2,1,0:T(8,128)(2,1)} %broadcast_in_dim.2), calls=%async_computation.1 | async-start | bytes 1048576 | tf_op jit(solution)/shard_map/all_to_all | solution.py:125
  40.5 0.0 collective-permute-done.2
  40.5 0.1 broadcast_select_fusion.1
  40.6 0.3 fusion
  40.9 0.3 fusion.1.lists_ref
  41.3 13.3 %all-to-all-done.1.points_ref = bf16[8,128,256]{2,1,0:T(8,128)(2,1)S(1)} async-done(((bf16[8,128,256]{2,1,0:T(8,128)(2,1)}), bf16[8,128,256]{2,1,0:T(8,128)(2,1)S(1)}, u32[]{:S(2)}, u32[]{:S(2)}) %all-to-all-start.1) | async-done | bytes 524320 | tf_op jit(solution)/shard_map/all_to_all | solution.py:125
  54.6 2.7 %energy.1 = (bf16[2048,1024]{1,0:T(8,128)(2,1)S(1)}, f32[32,16,128]{2,1,0:T(8,128)S(1)}) custom-call(bf16[8,128,256]{2,1,0:T(8,128)(2,1)S(1)} %all-to-all-done.1.points_ref, bf16[2048,256]{1,0:T(8,128)(2,1)S(1)} %fusion.1.lists_ref), custom_call_target="tpu_custom_call" | custom-call | tf_op jit(solution)/shard_map/energy/pallas_call | solution.py:150
  57.3 0.0 copy-start
  57.3 17.9 %all_to_all.45.parts_ref = f32[32,16,128]{2,1,0:T(8,128)S(1)} all-to-all(f32[32,16,128]{2,1,0:T(8,128)S(1)} %get-tuple-element.6), channel_id=1, replica_groups=mesh['x'=4,'yl'=2,'c'=2,'z'=8,'yh'=2] {'x','yl','c','yh'}, dimensions={0} | all-to-all | bytes 524288 | tf_op jit(solution)/shard_map/all_to_all | solution.py:159
  75.2 0.7 row_sums.3
  75.8 9.2 %all_to_all.46.parts_ref = f32[8,8,128]{2,1,0:T(8,128)S(1)} all-to-all(f32[8,8,128]{2,1,0:T(8,128)S(1)} %row_sums.3), channel_id=1, replica_groups=mesh['x'=4,'yl'=2,'c'=2,'z'=8,'yh'=2] {'z'}, dimensions={0} | all-to-all | bytes 65536 | tf_op jit(solution)/shard_map/all_to_all | solution.py:168
  85.1 1.2 column_sums.2
  86.3 13.4 %all_to_all.47.parts_ref = f32[32,16,128]{2,1,0:T(8,128)S(1)} all-to-all(f32[32,16,128]{2,1,0:T(8,128)S(1)} %column_sums.2), channel_id=1, replica_groups=mesh['x'=4,'yl'=2,'c'=2,'z'=8,'yh'=2] {'x','yl','c','yh'}, dimensions={0} | all-to-all | bytes 524288 | tf_op jit(solution)/shard_map/all_to_all | solution.py:159
  99.7 0.7 row_sums.4
  100.4 9.2 %all_to_all.48.parts_ref = f32[8,8,128]{2,1,0:T(8,128)S(1)} all-to-all(f32[8,8,128]{2,1,0:T(8,128)S(1)} %row_sums.4), channel_id=1, replica_groups=mesh['x'=4,'yl'=2,'c'=2,'z'=8,'yh'=2] {'z'}, dimensions={0} | all-to-all | bytes 65536 | tf_op jit(solution)/shard_map/all_to_all | solution.py:168
  109.6 1.2 column_sums.3
  110.8 13.4 %all_to_all.49.parts_ref.columns_ref = f32[32,16,128]{2,1,0:T(8,128)S(1)} all-to-all(f32[32,16,128]{2,1,0:T(8,128)S(1)} %column_sums.3), channel_id=1, replica_groups=mesh['x'=4,'yl'=2,'c'=2,'z'=8,'yh'=2] {'x','yl','c','yh'}, dimensions={0} | all-to-all | bytes 524288 | tf_op jit(solution)/shard_map/all_to_all | solution.py:159
  124.2 0.0 copy-done
  124.2 1.3 row_sums.5
  125.5 3.5 %all-to-all-start.7 = ((f32[8,8,128]{2,1,0:T(8,128)}), f32[8,8,128]{2,1,0:T(8,128)S(1)}, u32[]{:S(2)}, u32[]{:S(2)}) async-start(f32[8,8,128]{2,1,0:T(8,128)} %row_sums.5), calls=%async_computation.7 | async-start | bytes 65536 | tf_op jit(solution)/shard_map/all_to_all | solution.py:168
  129.0 6.6 %all-to-all-done.7.rows_ref = f32[8,8,128]{2,1,0:T(8,128)S(1)} async-done(((f32[8,8,128]{2,1,0:T(8,128)}), f32[8,8,128]{2,1,0:T(8,128)S(1)}, u32[]{:S(2)}, u32[]{:S(2)}) %all-to-all-start.7) | async-done | bytes 32800 | tf_op jit(solution)/shard_map/all_to_all | solution.py:168
  135.6 0.0 copy-start.1
  135.6 2.2 %copy-done.1 = bf16[2048,1024]{1,0:T(8,128)(2,1)S(1)} copy-done((bf16[2048,1024]{1,0:T(8,128)(2,1)S(1)}, bf16[2048,1024]{1,0:T(8,128)(2,1)}, u32[]{:S(2)}) %copy-start.1) | copy-done | bytes 4194328
  137.8 1.4 update.1
  139.3 1.7 %collective-permute-start.3 = (f32[16,64,256]{2,1,0:T(8,128)S(1)}, f32[16,64,256]{2,1,0:T(8,128)}, u32[]{:S(2)}, u32[]{:S(2)}) collective-permute-start(f32[16,64,256]{2,1,0:T(8,128)S(1)} %get-tuple-element.9), channel_id=1, source_target_pairs={{0,16},{16,0},{1,17},{17,1},{2,18},{18,2},{3,19},{19,3},{4,20},{20... | collective-permute-start | bytes 3145736 | tf_op jit(solution)/shard_map/ppermute | solution.py:189
  140.9 2.4 %collective-permute-done.3 = f32[16,64,256]{2,1,0:T(8,128)} collective-permute-done((f32[16,64,256]{2,1,0:T(8,128)S(1)}, f32[16,64,256]{2,1,0:T(8,128)}, u32[]{:S(2)}, u32[]{:S(2)}) %collective-permute-start.3) | collective-permute-done | bytes 1048608 | tf_op jit(solution)/shard_map/ppermute | solution.py:189
  143.4 2.1 %add_convert_fusion = bf16[16,64,256]{2,1,0:T(8,128)(2,1)} fusion(f32[16,64,256]{2,1,0:T(8,128)S(1)} %get-tuple-element.8, f32[16,64,256]{2,1,0:T(8,128)} %collective-permute-done.3), kind=kLoop, calls=%fused_computation.8 | loop fusion | flops 524288 | bytes 2621440 | tf_op jit(solution)/shard_map/convert_element_type | solution.py:190
  145.5 3.6 %all-to-all-start.8 = ((bf16[16,64,256]{2,1,0:T(8,128)(2,1)}), bf16[16,64,256]{2,1,0:T(8,128)(2,1)S(1)}, u32[]{:S(2)}, u32[]{:S(2)}) async-start(bf16[16,64,256]{2,1,0:T(8,128)(2,1)} %add_convert_fusion), calls=%async_computation.8 | async-start | bytes 1048576 | tf_op jit(solution)/shard_map/all_to_all | solution.py:190
  149.1 2.9 %collective-permute-start.4 = (f32[8,128]{1,0:T(8,128)S(1)}, f32[8,128]{1,0:T(8,128)S(1)}, u32[]{:S(2)}, u32[]{:S(2)}) collective-permute-start(f32[8,128]{1,0:T(8,128)S(1)} %divide_log_fusion), channel_id=1, source_target_pairs={{0,1},{1,0},{2,3},{3,2},{4,5},{5,4},{6,7},{7,6},{8,9},{9,8},{10,11... | collective-permute-start | bytes 12296 | tf_op jit(solution)/shard_map/ppermute | solution.py:180
  152.0 1.8 %collective-permute-done.4 = f32[8,128]{1,0:T(8,128)S(1)} collective-permute-done((f32[8,128]{1,0:T(8,128)S(1)}, f32[8,128]{1,0:T(8,128)S(1)}, u32[]{:S(2)}, u32[]{:S(2)}) %collective-permute-start.4) | collective-permute-done | bytes 4128 | tf_op jit(solution)/shard_map/ppermute | solution.py:180
  153.8 0.6 pad_maximum_fusion.1
  154.4 5.7 %all-to-all-done.8 = bf16[16,64,256]{2,1,0:T(8,128)(2,1)S(1)} async-done(((bf16[16,64,256]{2,1,0:T(8,128)(2,1)}), bf16[16,64,256]{2,1,0:T(8,128)(2,1)S(1)}, u32[]{:S(2)}, u32[]{:S(2)}) %all-to-all-start.8) | async-done | bytes 524320 | tf_op jit(solution)/shard_map/all_to_all | solution.py:190
  160.1 0.1 convert_reduce_fusion
  160.1 0.1 multiply_reduce_fusion.1
  160.3 0.7 broadcast_multiply_fusion
  (8 shorter events, 0.1 us)
Async XLA Ops:
  0.6 5.5 %copy-start.3 = (bf16[64,256]{1,0:T(8,128)(2,1)S(1)}, bf16[64,256]{1,0:T(8,128)(2,1)}, u32[]{:S(2)}) copy-start(bf16[64,256]{1,0:T(8,128)(2,1)} %param.4) | copy-start | bytes 98308
  0.6 5.9 %collective-permute-start.1 = (bf16[64,256]{1,0:T(8,128)(2,1)}, bf16[64,256]{1,0:T(8,128)(2,1)S(1)}, u32[]{:S(2)}, u32[]{:S(2)}) collective-permute-start(bf16[64,256]{1,0:T(8,128)(2,1)} %param.4), channel_id=1, source_target_pairs={{0,1},{1,0},{2,3},{3,2},{4,5},{5,4},{6,7},{7,6},{8,9},{9,8},{10,11... | collective-permute-start | bytes 98312 | tf_op jit(solution)/shard_map/ppermute | solution.py:134
  6.0 14.8 %copy-start.2 = (bf16[1024,256]{1,0:T(8,128)(2,1)S(1)}, bf16[1024,256]{1,0:T(8,128)(2,1)}, u32[]{:S(2)}) copy-start(bf16[1024,256]{1,0:T(8,128)(2,1)} %param.5) | copy-start | bytes 1572868
  6.1 5.4 %collective-permute-start = (bf16[64,1024]{1,0:T(8,128)(2,1)S(1)}, bf16[64,1024]{1,0:T(8,128)(2,1)S(1)}, u32[]{:S(2)}, u32[]{:S(2)}) collective-permute-start(bf16[64,1024]{1,0:T(8,128)(2,1)S(1)} %bitcast.26), channel_id=1, source_target_pairs={{0,1},{1,0},{2,3},{3,2},{4,5},{5,4},{6,7},{7,6},{8,9},{9,8},{10,11... | collective-permute-start | bytes 393224 | tf_op jit(solution)/shard_map/ppermute | solution.py:133
  12.6 23.3 %all-to-all-start = ((bf16[8,128,256]{2,1,0:T(8,128)(2,1)}), bf16[8,128,256]{2,1,0:T(8,128)(2,1)S(1)}, u32[]{:S(2)}, u32[]{:S(2)}) async-start(bf16[8,128,256]{2,1,0:T(8,128)(2,1)} %bitcast.2), calls=%async_computation | async-start | bytes 1048576 | tf_op jit(solution)/shard_map/all_to_all | solution.py:141
  20.8 19.7 %collective-permute-start.2 = (bf16[1024,256]{1,0:T(8,128)(2,1)S(1)}, bf16[1024,256]{1,0:T(8,128)(2,1)S(1)}, u32[]{:S(2)}, u32[]{:S(2)}) collective-permute-start(bf16[1024,256]{1,0:T(8,128)(2,1)S(1)} %copy-done.2), channel_id=1, source_target_pairs={{0,1},{1,0},{2,3},{3,2},{4,5},{5,4},{6,7},{7,6},{8,9},{9,8},{10,11... | collective-permute-start | bytes 1572872 | tf_op jit(solution)/shard_map/ppermute | solution.py:135
  37.0 17.6 %all-to-all-start.1 = ((bf16[8,128,256]{2,1,0:T(8,128)(2,1)}), bf16[8,128,256]{2,1,0:T(8,128)(2,1)S(1)}, u32[]{:S(2)}, u32[]{:S(2)}) async-start(bf16[8,128,256]{2,1,0:T(8,128)(2,1)} %broadcast_in_dim.2), calls=%async_computation.1 | async-start | bytes 1048576 | tf_op jit(solution)/shard_map/all_to_all | solution.py:125
  57.3 66.9 %copy-start = (bf16[2048,1024]{1,0:T(8,128)(2,1)}, bf16[2048,1024]{1,0:T(8,128)(2,1)S(1)}, u32[]{:S(2)}) copy-start(bf16[2048,1024]{1,0:T(8,128)(2,1)S(1)} %get-tuple-element.7.energy_ref) | copy-start | bytes 12582916
  125.5 10.1 %all-to-all-start.7 = ((f32[8,8,128]{2,1,0:T(8,128)}), f32[8,8,128]{2,1,0:T(8,128)S(1)}, u32[]{:S(2)}, u32[]{:S(2)}) async-start(f32[8,8,128]{2,1,0:T(8,128)} %row_sums.5), calls=%async_computation.7 | async-start | bytes 65536 | tf_op jit(solution)/shard_map/all_to_all | solution.py:168
  135.6 2.2 %copy-start.1 = (bf16[2048,1024]{1,0:T(8,128)(2,1)S(1)}, bf16[2048,1024]{1,0:T(8,128)(2,1)}, u32[]{:S(2)}) copy-start(bf16[2048,1024]{1,0:T(8,128)(2,1)} %copy-done) | copy-start | bytes 12582916
  139.3 4.1 %collective-permute-start.3 = (f32[16,64,256]{2,1,0:T(8,128)S(1)}, f32[16,64,256]{2,1,0:T(8,128)}, u32[]{:S(2)}, u32[]{:S(2)}) collective-permute-start(f32[16,64,256]{2,1,0:T(8,128)S(1)} %get-tuple-element.9), channel_id=1, source_target_pairs={{0,16},{16,0},{1,17},{17,1},{2,18},{18,2},{3,19},{19,3},{4,20},{20... | collective-permute-start | bytes 3145736 | tf_op jit(solution)/shard_map/ppermute | solution.py:189
  145.5 14.6 %all-to-all-start.8 = ((bf16[16,64,256]{2,1,0:T(8,128)(2,1)}), bf16[16,64,256]{2,1,0:T(8,128)(2,1)S(1)}, u32[]{:S(2)}, u32[]{:S(2)}) async-start(bf16[16,64,256]{2,1,0:T(8,128)(2,1)} %add_convert_fusion), calls=%async_computation.8 | async-start | bytes 1048576 | tf_op jit(solution)/shard_map/all_to_all | solution.py:190
  149.1 4.7 %collective-permute-start.4 = (f32[8,128]{1,0:T(8,128)S(1)}, f32[8,128]{1,0:T(8,128)S(1)}, u32[]{:S(2)}, u32[]{:S(2)}) collective-permute-start(f32[8,128]{1,0:T(8,128)S(1)} %divide_log_fusion), channel_id=1, source_target_pairs={{0,1},{1,0},{2,3},{3,2},{4,5},{5,4},{6,7},{7,6},{8,9},{9,8},{10,11... | collective-permute-start | bytes 12296 | tf_op jit(solution)/shard_map/ppermute | solution.py:180

commit v3 on v2

--- a/solution.py
+++ b/solution.py
@@ -52,9 +52,9 @@
 
 
 def add_parts(ref):
-    tile = ref[0]
+    tile = ref[0].astype(f32)
     for k in range(1, ref.shape[0]):
-        tile += ref[k]
+        tile += ref[k].astype(f32)
     return tile
 
 
@@ -67,6 +67,27 @@
             preferred_element_type=f32,
         )
     )
+
+
+def hidden_kernel(core_ref, parts_ref, columns_ref, out_ref):
+    core = core_ref[0]
+    contract = (((0,), (0,)), ((), ()))
+    tower = parts_ref[:, :64, :].reshape(1024, ROWS)
+    kept = parts_ref[:, 64:, :].reshape(1024, 128)
+    taken = columns_ref[...].reshape(1024, 128)
+    low = jnp.where(core == 0, kept, taken)
+    high = jnp.where(core == 0, taken, kept)
+    hidden = lax.dot_general(
+        tower, jnp.concatenate([low, high], axis=1), contract, preferred_element_type=f32
+    )
+    out_ref[...] = jnp.broadcast_to(rms_norm(hidden).astype(bf16)[None], out_ref.shape)
+
+
+def finish_kernel(parts_ref, out_ref):
+    sums = parts_ref[0].astype(f32)
+    for k in range(1, 16):
+        sums += parts_ref[k].astype(f32)
+    out_ref[...] = rms_norm(sums)
 
 
 def energy_kernel(points_ref, lists_ref, energy_ref, column_ref):
@@ -78,7 +99,7 @@
         )
         energy_ref[rows, :] = jnp.exp(scores * (1.0 / (DP * temper)) - 1.0 / temper).astype(bf16)
     local = column_sums(jnp.ones((8, 128), f32), energy_ref[...])
-    column_ref[...] = jnp.broadcast_to(local[None], column_ref.shape)
+    column_ref[...] = jnp.broadcast_to(local.astype(bf16)[None], column_ref.shape)
 
 
 def row_kernel(parts_ref, energy_ref, row_ref):
@@ -91,16 +112,17 @@
 
 def column_kernel(parts_ref, energy_ref, column_ref):
     local = column_sums(1.0 / add_parts(parts_ref), energy_ref[...])
-    column_ref[...] = jnp.broadcast_to(local[None], column_ref.shape)
+    column_ref[...] = jnp.broadcast_to(local.astype(bf16)[None], column_ref.shape)
 
 
 def down_lanes(row):
     return jnp.transpose(jnp.broadcast_to(row, (128, 128)))
 
 
-def update_kernel(core_ref, rows_ref, columns_ref, energy_ref, points_ref, mine_ref, other_ref):
+def update_kernel(core_ref, rows_ref, columns_ref, energy_ref, points_ref, mine_ref, other_ref, log_ref):
     core = core_ref[0]
     row_scale = 1.0 / add_parts(rows_ref)
+    log_ref[...] = jnp.log(row_scale)
     col_scale = 2.0 / add_parts(columns_ref)
     scaled = []
     for k in range(8):
@@ -114,42 +136,40 @@
             energy_ref[pl.ds(128 * k, 128), :], scaled, preferred_element_type=f32
         ) * jnp.concatenate([factor, factor], axis=1)
         mine_ref[k] = jnp.where(core == 0, sums[:64], sums[64:])
-        other_ref[k] = jnp.where(core == 0, sums[64:], sums[:64])
-
-
-def parts_shape(count, rows):
-    return jax.ShapeDtypeStruct((count, rows, 128), f32)
-
-
-def gather_all(values, axis, size):
-    return lax.all_to_all(jnp.broadcast_to(values[None], (size,) + values.shape), axis, 0, 0)
+        other_ref[k] = jnp.where(core == 0, sums[64:], sums[:64]).astype(bf16)
+
+
+def parts_shape(count, rows, dtype):
+    return jax.ShapeDtypeStruct((count, rows, 128), dtype)
 
 
 def on_device(tower_out, projection, centroids):
     half = lax.axis_index("yh")
-    tower = tower_out.T.reshape(64, 8, 2, ROWS)
-    kept = jnp.where(half == 0, tower[:, :, 0], tower[:, :, 1]).reshape(64, 8 * ROWS)
-    given = jnp.where(half == 0, tower[:, :, 1], tower[:, :, 0]).reshape(64, 8 * ROWS)
-    taken = lax.ppermute(given, "yh", SWAP)
-    taken_projection = lax.ppermute(projection, "yh", SWAP)
+    core = lax.axis_index("c")
+    core_index = core.reshape(1)
+    tower = tower_out.T.reshape(64, 16, ROWS).transpose(1, 0, 2)
+    columns = jnp.where(core == 0, projection[:, :128], projection[:, 128:])
+    message = jnp.concatenate([tower, jnp.broadcast_to(columns[None], (16, 64, 128))], axis=1)
+    parts = lax.all_to_all(message, ("z", "yh"), 0, 0)
+    taken_columns = lax.ppermute(parts[:, 64:], "c", SWAP)
+    spread = pl.pallas_call(
+        hidden_kernel,
+        out_shape=jax.ShapeDtypeStruct((8, ROWS, DP), bf16),
+        in_specs=[pl.BlockSpec(memory_space=pltpu.SMEM)] + whole(2),
+        out_specs=whole(1)[0],
+        compiler_params=LIMIT,
+        name="hidden",
+    )(core_index, parts, taken_columns)
+    points = lax.all_to_all(spread, "z", 0, 0)
+
     taken_centroids = lax.ppermute(centroids, "yh", SWAP)
-
-    contract = (((0,), (0,)), ((), ()))
-    partial = lax.dot_general(kept, projection, contract, preferred_element_type=f32)
-    partial += lax.dot_general(taken, taken_projection, contract, preferred_element_type=f32)
-    partial = partial.astype(bf16).reshape(8, ROWS, DP)
-    shares = lax.all_to_all(partial, "z", 0, 0)
-    hidden = jnp.sum(shares.astype(f32), axis=0)
-    own = rms_norm(hidden).astype(bf16)
-    points = gather_all(own, "z", 8)
-
     low = jnp.where(half == 0, centroids, taken_centroids)
     high = jnp.where(half == 0, taken_centroids, centroids)
     unit_lists = rms_norm(jnp.concatenate([low, high]).astype(f32)).astype(bf16)
 
     energy, columns = pl.pallas_call(
         energy_kernel,
-        out_shape=(VMEM((2048, 1024), bf16), parts_shape(32, 16)),
+        out_shape=(VMEM((2048, 1024), bf16), parts_shape(32, 16, bf16)),
         in_specs=whole(2),
         out_specs=whole(2),
         compiler_params=LIMIT,
@@ -159,7 +179,7 @@
         columns = lax.all_to_all(columns, PLANE, 0, 0)
         rows = pl.pallas_call(
             row_kernel,
-            out_shape=parts_shape(8, 8),
+            out_shape=parts_shape(8, 8, f32),
             in_specs=whole(2),
             out_specs=whole(1)[0],
             compiler_params=LIMIT,
@@ -169,30 +189,41 @@
         if sweep < ITERS - 1:
             columns = pl.pallas_call(
                 column_kernel,
-                out_shape=parts_shape(32, 16),
+                out_shape=parts_shape(32, 16, bf16),
                 in_specs=whole(2),
                 out_specs=whole(1)[0],
                 compiler_params=LIMIT,
                 name="column_sums",
             )(rows, stay(energy))
 
-    row_log = jnp.log(1.0 / jnp.sum(rows, axis=0))
+    mine, other, row_log = pl.pallas_call(
+        update_kernel,
+        out_shape=(
+            jax.ShapeDtypeStruct((16, 64, DP), f32),
+            jax.ShapeDtypeStruct((16, 64, DP), bf16),
+            jax.ShapeDtypeStruct((8, 128), f32),
+        ),
+        in_specs=[pl.BlockSpec(memory_space=pltpu.SMEM)] + whole(4),
+        out_specs=whole(3),
+        compiler_params=LIMIT,
+        name="update",
+    )(core_index, rows, columns, stay(energy), points)
+    mine += lax.ppermute(other, "c", SWAP).astype(f32)
+    owned = lax.all_to_all(mine.astype(bf16), CHIPS, 0, 0)
+    refreshed = pl.pallas_call(
+        finish_kernel,
+        out_shape=jax.ShapeDtypeStruct((64, DP), f32),
+        in_specs=whole(1),
+        out_specs=whole(1)[0],
+        compiler_params=LIMIT,
+        name="finish",
+    )(owned)
+
     taken_log = lax.ppermute(row_log, "yh", SWAP)
-    mine, other = pl.pallas_call(
-        update_kernel,
-        out_shape=(jax.ShapeDtypeStruct((16, 64, DP), f32),) * 2,
-        in_specs=[pl.BlockSpec(memory_space=pltpu.SMEM)] + whole(4),
-        out_specs=whole(2),
-        compiler_params=LIMIT,
-        name="update",
-    )(lax.axis_index("c").reshape(1), rows, columns, stay(energy), points)
-    mine += lax.ppermute(other, "c", SWAP)
-    owned = jnp.sum(lax.all_to_all(mine.astype(bf16), CHIPS, 0, 0).astype(f32), axis=0)
-
     low_log = jnp.where(half == 0, row_log, taken_log)
     high_log = jnp.where(half == 0, taken_log, row_log)
     row_log = jnp.stack([low_log, high_log], axis=1).reshape(16 * ROWS)
-    return (rms_norm(owned), row_log)
+    return (refreshed, row_log)
 
 
 def solution(mesh):

time: 162 us -> 152 us (0.938)
  waiting for transfers between devices: 49.7 us -> 41.6 us
  local copies, waits for them, and re-layouts: 4.52 us -> 1.66 us
  blocking collectives: 63.2 us -> 64.9 us
    all_to_all x2 -> x3, blocking collectives: 18.5 us -> 27.8 us  [on_device(): rows = lax.all_to_all(rows, 'z', 0, 0)]
    all_to_all x3, blocking collectives: 44.7 us -> 37.2 us  [on_device(): columns = lax.all_to_all(columns, PLANE, 0, 0)]
    ppermute x3 -> x2, waiting for transfers between devices: 7.36 us -> 2.7 us  [the longest x1 1.54 us: on_device(): mine += lax.ppermute(other, 'c', SWAP).astype(f32)]
    all_to_all x4 -> x3, waiting for transfers between devices: 40.5 us -> 37 us  [the longest x1 17.1 us: on_device(): points = lax.all_to_all(spread, 'z', 0, 0)]
    ppermute x1, starting transfers between devices: 0.14 us -> 2.95 us  [on_device(): taken_centroids = lax.ppermute(centroids, 'yh', SWAP)]
    pallas_call x5 -> x7, Pallas kernels: 5.06 us -> 6.4 us  [the longest x2 2.42 us: on_device(): pl.pallas_call(column_kernel, out_shape=parts_shape(32, 16, bf16), in_spe...]
    ppermute x3 -> x2, starting transfers between devices: 5.6 us -> 4.34 us  [the longest x1 2.57 us: on_device(): taken_columns = lax.ppermute(parts[:, 64:], 'c', SWAP)]
    all_to_all x4 -> x3, starting transfers between devices: 18.8 us -> 18.8 us  [the longest x1 11.7 us: on_device(): parts = lax.all_to_all(message, ('z', 'yh'), 0, 0)]
  transfers between devices with their start and end apart: 9 -> 7, of which waited for: 7 -> 6; matrix products, arithmetic and copies ran while one was open for 3% -> 1% of each run, Pallas kernels for 0% -> 1%
where the time goes in v3:
time: 152 us
  blocking collectives  64.9 us (43%)
  waiting for transfers between devices  41.6 us (27%)
  starting transfers between devices  28.9 us (19%)
  Pallas kernels  10.6 us (7%)
  other arithmetic  3.31 us (2%)
  local copies, waits for them, and re-layouts  1.66 us (1%)
    all_to_all x3, blocking collectives, on_device(): columns = lax.all_to_all(columns, PLANE, 0, 0)  37.2 us
    all_to_all x3, blocking collectives, on_device(): rows = lax.all_to_all(rows, 'z', 0, 0)  27.8 us
    all_to_all x1, waiting for transfers between devices, on_device(): points = lax.all_to_all(spread, 'z', 0, 0)  17.1 us
    all_to_all x1, waiting for transfers between devices, on_device(): parts = lax.all_to_all(message, ('z', 'yh'), 0, 0)  14.2 us
    all_to_all x1, starting transfers between devices, on_device(): parts = lax.all_to_all(message, ('z', 'yh'), 0, 0)  11.7 us
    all_to_all x1, waiting for transfers between devices, on_device(): owned = lax.all_to_all(mine.astype(bf16), CHIPS, 0, 0)  5.66 us
    all_to_all x1, starting transfers between devices, on_device(): owned = lax.all_to_all(mine.astype(bf16), CHIPS, 0, 0)  3.57 us
    all_to_all x1, starting transfers between devices, on_device(): points = lax.all_to_all(spread, 'z', 0, 0)  3.49 us
  transfers between devices with their start and end apart: 7, of which 6 were waited for; matrix products, arithmetic and copies ran while one was open for 1% of the time, Pallas kernels for 1%

profile of v3, /device:TPU:1, one launch (start us, length us, event | category | flops | bytes accessed | tf_op | source)
XLA Modules:
  0.0 151.8 jit_solution(17103807581758829112)
XLA Ops:
  0.6 0.0 copy-start
  0.6 0.0 copy-start.1
  0.7 0.9 copy-done
  1.6 0.1 bitcast_bitcast_fusion
  1.7 0.7 slice_select_fusion
  2.5 0.8 pad_maximum_fusion.1
  3.3 11.7 %all-to-all-start = ((bf16[16,128,128]{2,1,0:T(8,128)(2,1)}), bf16[16,128,128]{2,1,0:T(8,128)(2,1)S(1)}, u32[]{:S(2)}, u32[]{:S(2)}) async-start(bf16[16,128,128]{2,1,0:T(8,128)(2,1)} %pad_maximum_fusion.1), calls=%async_computation | async-start | bytes 1048576 | tf_op jit(solution)/shard_map/all_to_all | solution.py:153
  15.0 0.0 copy-done.1
  15.1 3.0 %collective-permute-start.1 = (bf16[1024,256]{1,0:T(8,128)(2,1)S(1)}, bf16[1024,256]{1,0:T(8,128)(2,1)S(1)}, u32[]{:S(2)}, u32[]{:S(2)}) collective-permute-start(bf16[1024,256]{1,0:T(8,128)(2,1)S(1)} %copy-done.1), channel_id=1, source_target_pairs={{0,1},{1,0},{2,3},{3,2},{4,5},{5,4},{6,7},{7,6},{8,9},{9,8},{10,11... | collective-permute-start | bytes 1572872 | tf_op jit(solution)/shard_map/ppermute | solution.py:165
  18.0 14.2 %all-to-all-done.parts_ref = bf16[16,128,128]{2,1,0:T(8,128)(2,1)S(1)} async-done(((bf16[16,128,128]{2,1,0:T(8,128)(2,1)}), bf16[16,128,128]{2,1,0:T(8,128)(2,1)S(1)}, u32[]{:S(2)}, u32[]{:S(2)}) %all-to-all-start) | async-done | bytes 524320 | tf_op jit(solution)/shard_map/all_to_all | solution.py:153
  32.2 2.6 %collective-permute-start = (bf16[16,64,128]{2,1,0:T(8,128)(2,1)S(1)}, bf16[16,64,128]{2,1,0:T(8,128)(2,1)S(1)}, u32[]{:S(2)}, u32[]{:S(2)}) collective-permute-start(bf16[16,64,128]{2,1,0:T(8,128)(2,1)S(1)} %slice.12), channel_id=1, source_target_pairs={{0,16},{16,0},{1,17},{17,1},{2,18},{18,2},{3,19},{19,3},{4,20},{20... | collective-permute-start | bytes 786440 | tf_op jit(solution)/shard_map/ppermute | solution.py:154
  34.8 1.2 collective-permute-done.columns_ref
  35.9 1.2 hidden.1
  37.1 3.5 %all-to-all-start.1 = ((bf16[8,128,256]{2,1,0:T(8,128)(2,1)}), bf16[8,128,256]{2,1,0:T(8,128)(2,1)S(1)}, u32[]{:S(2)}, u32[]{:S(2)}) async-start(bf16[8,128,256]{2,1,0:T(8,128)(2,1)} %hidden.1), calls=%async_computation.1 | async-start | bytes 1048576 | tf_op jit(solution)/shard_map/all_to_all | solution.py:163
  40.6 0.0 collective-permute-done.1
  40.6 0.1 broadcast_select_fusion.1
  40.7 0.3 fusion
  41.1 0.3 fusion.1.lists_ref
  41.4 17.1 %all-to-all-done.1.points_ref = bf16[8,128,256]{2,1,0:T(8,128)(2,1)S(1)} async-done(((bf16[8,128,256]{2,1,0:T(8,128)(2,1)}), bf16[8,128,256]{2,1,0:T(8,128)(2,1)S(1)}, u32[]{:S(2)}, u32[]{:S(2)}) %all-to-all-start.1) | async-done | bytes 524320 | tf_op jit(solution)/shard_map/all_to_all | solution.py:163
  58.5 2.7 %energy.1 = (bf16[2048,1024]{1,0:T(8,128)(2,1)S(1)}, bf16[32,16,128]{2,1,0:T(8,128)(2,1)S(1)}) custom-call(bf16[8,128,256]{2,1,0:T(8,128)(2,1)S(1)} %all-to-all-done.1.points_ref, bf16[2048,256]{1,0:T(8,128)(2,1)S(1)} %fusion.1.lists_ref), custom_call_target="tpu_custom_call" | custom-call | tf_op jit(solution)/shard_map/energy/pallas_call | solution.py:170
  61.2 12.5 %all_to_all.45.parts_ref = bf16[32,16,128]{2,1,0:T(8,128)(2,1)S(1)} all-to-all(bf16[32,16,128]{2,1,0:T(8,128)(2,1)S(1)} %get-tuple-element.7), channel_id=1, replica_groups=mesh['x'=4,'yl'=2,'c'=2,'z'=8,'yh'=2] {'x','yl','c','yh'}, dimensions={0} | all-to-all | bytes 262144 | tf_op jit(solution)/shard_map/all_to_all | solution.py:179
  73.7 0.7 row_sums.3
  74.4 9.3 %all_to_all.46.parts_ref = f32[8,8,128]{2,1,0:T(8,128)S(1)} all-to-all(f32[8,8,128]{2,1,0:T(8,128)S(1)} %row_sums.3), channel_id=1, replica_groups=mesh['x'=4,'yl'=2,'c'=2,'z'=8,'yh'=2] {'z'}, dimensions={0} | all-to-all | bytes 65536 | tf_op jit(solution)/shard_map/all_to_all | solution.py:188
  83.6 1.2 column_sums.2
  84.9 12.4 %all_to_all.47.parts_ref = bf16[32,16,128]{2,1,0:T(8,128)(2,1)S(1)} all-to-all(bf16[32,16,128]{2,1,0:T(8,128)(2,1)S(1)} %column_sums.2), channel_id=1, replica_groups=mesh['x'=4,'yl'=2,'c'=2,'z'=8,'yh'=2] {'x','yl','c','yh'}, dimensions={0} | all-to-all | bytes 262144 | tf_op jit(solution)/shard_map/all_to_all | solution.py:179
  97.2 0.7 row_sums.4
  97.9 9.3 %all_to_all.48.parts_ref = f32[8,8,128]{2,1,0:T(8,128)S(1)} all-to-all(f32[8,8,128]{2,1,0:T(8,128)S(1)} %row_sums.4), channel_id=1, replica_groups=mesh['x'=4,'yl'=2,'c'=2,'z'=8,'yh'=2] {'z'}, dimensions={0} | all-to-all | bytes 65536 | tf_op jit(solution)/shard_map/all_to_all | solution.py:188
  107.1 1.2 column_sums.3
  108.4 12.4 %all_to_all.49.parts_ref.columns_ref = bf16[32,16,128]{2,1,0:T(8,128)(2,1)S(1)} all-to-all(bf16[32,16,128]{2,1,0:T(8,128)(2,1)S(1)} %column_sums.3), channel_id=1, replica_groups=mesh['x'=4,'yl'=2,'c'=2,'z'=8,'yh'=2] {'x','yl','c','yh'}, dimensions={0} | all-to-all | bytes 262144 | tf_op jit(solution)/shard_map/all_to_all | solution.py:179
  120.7 0.7 row_sums.5
  121.4 9.3 %all_to_all.50.rows_ref = f32[8,8,128]{2,1,0:T(8,128)S(1)} all-to-all(f32[8,8,128]{2,1,0:T(8,128)S(1)} %row_sums.5), channel_id=1, replica_groups=mesh['x'=4,'yl'=2,'c'=2,'z'=8,'yh'=2] {'z'}, dimensions={0} | all-to-all | bytes 65536 | tf_op jit(solution)/shard_map/all_to_all | solution.py:188
  130.6 1.5 %update.1 = (f32[16,64,256]{2,1,0:T(8,128)S(1)}, bf16[16,64,256]{2,1,0:T(8,128)(2,1)S(1)}, f32[8,128]{1,0:T(8,128)S(1)}) custom-call(s32[1]{0:T(128)} %bitcast.core_ref, f32[8,8,128]{2,1,0:T(8,128)S(1)} %all_to_all.50.rows_ref, bf16[32,16,128]{2,1,0:T(8,128)(2,1)S(1)} %all_to_all.49.parts_ref.columns_ref, ...), custom_call_target="tpu_custom_call" | custom-call | tf_op jit(solution)/shard_map/update/pallas_call | solution.py:199
  132.2 1.8 %collective-permute-start.2 = (bf16[16,64,256]{2,1,0:T(8,128)(2,1)S(1)}, bf16[16,64,256]{2,1,0:T(8,128)(2,1)S(1)}, u32[]{:S(2)}, u32[]{:S(2)}) collective-permute-start(bf16[16,64,256]{2,1,0:T(8,128)(2,1)S(1)} %get-tuple-element.10), channel_id=1, source_target_pairs={{0,16},{16,0},{1,17},{17,1},{2,18},{18,2},{3,19},{19,3},{4,20},{20... | collective-permute-start | bytes 1572872 | tf_op jit(solution)/shard_map/ppermute | solution.py:211
  133.9 1.5 %collective-permute-done.2 = bf16[16,64,256]{2,1,0:T(8,128)(2,1)S(1)} collective-permute-done((bf16[16,64,256]{2,1,0:T(8,128)(2,1)S(1)}, bf16[16,64,256]{2,1,0:T(8,128)(2,1)S(1)}, u32[]{:S(2)}, u32[]{:S(2)}) %collective-permute-start.2) | collective-permute-done | bytes 524320 | tf_op jit(solution)/shard_map/ppermute | solution.py:211
  135.5 1.0 add_convert_fusion
  136.4 3.6 %all-to-all-start.8 = ((bf16[16,64,256]{2,1,0:T(8,128)(2,1)}), bf16[16,64,256]{2,1,0:T(8,128)(2,1)S(1)}, u32[]{:S(2)}, u32[]{:S(2)}) async-start(bf16[16,64,256]{2,1,0:T(8,128)(2,1)} %add_convert_fusion), calls=%async_computation.8 | async-start | bytes 1048576 | tf_op jit(solution)/shard_map/all_to_all | solution.py:212
  140.0 2.8 %collective-permute-start.3 = (f32[8,128]{1,0:T(8,128)S(1)}, f32[8,128]{1,0:T(8,128)S(1)}, u32[]{:S(2)}, u32[]{:S(2)}) collective-permute-start(f32[8,128]{1,0:T(8,128)S(1)} %get-tuple-element.11), channel_id=1, source_target_pairs={{0,1},{1,0},{2,3},{3,2},{4,5},{5,4},{6,7},{7,6},{8,9},{9,8},{10,11... | collective-permute-start | bytes 12296 | tf_op jit(solution)/shard_map/ppermute | solution.py:222
  142.8 1.9 %collective-permute-done.3 = f32[8,128]{1,0:T(8,128)S(1)} collective-permute-done((f32[8,128]{1,0:T(8,128)S(1)}, f32[8,128]{1,0:T(8,128)S(1)}, u32[]{:S(2)}, u32[]{:S(2)}) %collective-permute-start.3) | collective-permute-done | bytes 4128 | tf_op jit(solution)/shard_map/ppermute | solution.py:222
  144.7 0.6 copy.6
  145.3 5.7 %all-to-all-done.8.parts_ref = bf16[16,64,256]{2,1,0:T(8,128)(2,1)S(1)} async-done(((bf16[16,64,256]{2,1,0:T(8,128)(2,1)}), bf16[16,64,256]{2,1,0:T(8,128)(2,1)S(1)}, u32[]{:S(2)}, u32[]{:S(2)}) %all-to-all-start.8) | async-done | bytes 524320 | tf_op jit(solution)/shard_map/all_to_all | solution.py:212
  151.0 0.8 finish.1
  (5 shorter events, 0.1 us)
Async XLA Ops:
  0.6 1.0 copy-start
  0.6 14.4 %copy-start.1 = (bf16[1024,256]{1,0:T(8,128)(2,1)S(1)}, bf16[1024,256]{1,0:T(8,128)(2,1)}, u32[]{:S(2)}) copy-start(bf16[1024,256]{1,0:T(8,128)(2,1)} %param.5) | copy-start | bytes 1572868
  3.3 28.9 %all-to-all-start = ((bf16[16,128,128]{2,1,0:T(8,128)(2,1)}), bf16[16,128,128]{2,1,0:T(8,128)(2,1)S(1)}, u32[]{:S(2)}, u32[]{:S(2)}) async-start(bf16[16,128,128]{2,1,0:T(8,128)(2,1)} %pad_maximum_fusion.1), calls=%async_computation | async-start | bytes 1048576 | tf_op jit(solution)/shard_map/all_to_all | solution.py:153
  15.1 25.5 %collective-permute-start.1 = (bf16[1024,256]{1,0:T(8,128)(2,1)S(1)}, bf16[1024,256]{1,0:T(8,128)(2,1)S(1)}, u32[]{:S(2)}, u32[]{:S(2)}) collective-permute-start(bf16[1024,256]{1,0:T(8,128)(2,1)S(1)} %copy-done.1), channel_id=1, source_target_pairs={{0,1},{1,0},{2,3},{3,2},{4,5},{5,4},{6,7},{7,6},{8,9},{9,8},{10,11... | collective-permute-start | bytes 1572872 | tf_op jit(solution)/shard_map/ppermute | solution.py:165
  32.2 3.7 %collective-permute-start = (bf16[16,64,128]{2,1,0:T(8,128)(2,1)S(1)}, bf16[16,64,128]{2,1,0:T(8,128)(2,1)S(1)}, u32[]{:S(2)}, u32[]{:S(2)}) collective-permute-start(bf16[16,64,128]{2,1,0:T(8,128)(2,1)S(1)} %slice.12), channel_id=1, source_target_pairs={{0,16},{16,0},{1,17},{17,1},{2,18},{18,2},{3,19},{19,3},{4,20},{20... | collective-permute-start | bytes 786440 | tf_op jit(solution)/shard_map/ppermute | solution.py:154
  37.1 21.4 %all-to-all-start.1 = ((bf16[8,128,256]{2,1,0:T(8,128)(2,1)}), bf16[8,128,256]{2,1,0:T(8,128)(2,1)S(1)}, u32[]{:S(2)}, u32[]{:S(2)}) async-start(bf16[8,128,256]{2,1,0:T(8,128)(2,1)} %hidden.1), calls=%async_computation.1 | async-start | bytes 1048576 | tf_op jit(solution)/shard_map/all_to_all | solution.py:163
  132.2 3.3 %collective-permute-start.2 = (bf16[16,64,256]{2,1,0:T(8,128)(2,1)S(1)}, bf16[16,64,256]{2,1,0:T(8,128)(2,1)S(1)}, u32[]{:S(2)}, u32[]{:S(2)}) collective-permute-start(bf16[16,64,256]{2,1,0:T(8,128)(2,1)S(1)} %get-tuple-element.10), channel_id=1, source_target_pairs={{0,16},{16,0},{1,17},{17,1},{2,18},{18,2},{3,19},{19,3},{4,20},{20... | collective-permute-start | bytes 1572872 | tf_op jit(solution)/shard_map/ppermute | solution.py:211
  136.4 14.6 %all-to-all-start.8 = ((bf16[16,64,256]{2,1,0:T(8,128)(2,1)}), bf16[16,64,256]{2,1,0:T(8,128)(2,1)S(1)}, u32[]{:S(2)}, u32[]{:S(2)}) async-start(bf16[16,64,256]{2,1,0:T(8,128)(2,1)} %add_convert_fusion), calls=%async_computation.8 | async-start | bytes 1048576 | tf_op jit(solution)/shard_map/all_to_all | solution.py:212
  140.0 4.7 %collective-permute-start.3 = (f32[8,128]{1,0:T(8,128)S(1)}, f32[8,128]{1,0:T(8,128)S(1)}, u32[]{:S(2)}, u32[]{:S(2)}) collective-permute-start(f32[8,128]{1,0:T(8,128)S(1)} %get-tuple-element.11), channel_id=1, source_target_pairs={{0,1},{1,0},{2,3},{3,2},{4,5},{5,4},{6,7},{7,6},{8,9},{9,8},{10,11... | collective-permute-start | bytes 12296 | tf_op jit(solution)/shard_map/ppermute | solution.py:222

commit v4 on v1

v4 whole, which is shorter than its diff:
```python
import math

import jax
import jax.numpy as jnp
from jax import lax
from jax.experimental import pallas as pl
from jax.experimental.pallas import tpu as pltpu
from jax.sharding import Mesh, PartitionSpec as P

DP = 256
ITERS = 3
ROWS = 128

temper = 0.05
SLOPE = math.log2(math.e) / (DP * temper)
OFFSET = math.log2(math.e) / temper
SWAP = [(0, 1), (1, 0)]
CHIPS = ("yh", "x", "yl")
LISTS = ("z", "c")
bf16 = jnp.bfloat16
f32 = jnp.float32
VMEM = pltpu.VMEM
SCALAR = pl.BlockSpec(memory_space=pltpu.SMEM)
LIMIT = pltpu.CompilerParams(vmem_limit_bytes=40 * 2**20)
COST = pl.CostEstimate(flops=2**29, bytes_accessed=2**22, transcendentals=2**20)


def whole(count):
    return [pl.BlockSpec(memory_space=VMEM)] * count


def stay(array):
    return pltpu.with_memory_space_constraint(array, VMEM)


def far(array):
    return pltpu.with_memory_space_constraint(array, pltpu.HBM)


def call(kernel, out_shape, name, scalars, count, scratch=(), cost=None):
    single = not isinstance(out_shape, tuple)
    return pl.pallas_call(
        kernel,
        out_shape=out_shape,
        in_specs=[SCALAR] * scalars + whole(count),
        out_specs=whole(1)[0] if single else whole(len(out_shape)),
        scratch_shapes=scratch,
        compiler_params=LIMIT,
        cost_estimate=cost,
        name=name,
    )


def rms_norm(values):
    return values * lax.rsqrt(jnp.mean(values * values, axis=-1, keepdims=True) + 1e-06)


def split_rows(row):
    high = row.astype(bf16).astype(f32)
    index = lax.broadcasted_iota(jnp.int32, (16, row.shape[1]), 0)
    lhs = jnp.where(index == 0, high, jnp.where(index == 1, row - high, 0.0))
    return lhs.astype(bf16)


def to_lanes(tile):
    return jnp.concatenate([tile[k : k + 1] for k in range(tile.shape[0])], axis=1)


def to_tile(rows):
    line = rows[0:1] + rows[1:2]
    return jnp.concatenate(
        [line[:, 128 * k : 128 * (k + 1)] for k in range(line.shape[1] // 128)], axis=0
    )


def add_parts(ref):
    tile = ref[0].astype(f32)
    for k in range(1, ref.shape[0]):
        tile += ref[k].astype(f32)
    return tile


def spread(ref, tile):
    ref[...] = jnp.broadcast_to(tile.astype(ref.dtype)[None], ref.shape)


def by_core(core, own, other):
    return jnp.where(core == 0, own, other), jnp.where(core == 0, other, own)


def column_rows(scale, energy_t):
    return lax.dot_general(
        split_rows(to_lanes(scale)),
        energy_t,
        (((1,), (1,)), ((), ())),
        preferred_element_type=f32,
    )


def pack_kernel(core_ref, tower_ref, projection_ref, out_ref, tower, columns, sems):
    start = pl.multiple_of(core_ref[0] * 128, 128)
    copies = (
        pltpu.make_async_copy(tower_ref, tower, sems.at[0]),
        pltpu.make_async_copy(projection_ref.at[:, pl.ds(start, 128)], columns, sems.at[1]),
    )
    for copy in copies:
        copy.start()
    copies[1].wait()
    for k in range(16):
        out_ref[k, 64:, :] = columns[...]
    copies[0].wait()
    for k in range(16):
        out_ref[k, :64, :] = tower[:, ROWS * k : ROWS * (k + 1)]


def lists_kernel(half_ref, kept_ref, taken_ref, out_ref):
    half = half_ref[0]
    for lists_ref, index in ((kept_ref, half), (taken_ref, 1 - half)):
        rows = pl.ds(pl.multiple_of(512 * index, 512), 512)
        out_ref[rows, :] = rms_norm(lists_ref[...].astype(f32)).astype(bf16)


def hidden_kernel(core_ref, parts_ref, columns_ref, out_ref):
    contract = (((0,), (0,)), ((), ()))
    tower = parts_ref[:, :64, :].reshape(1024, ROWS)
    kept = parts_ref[:, 64:, :].reshape(1024, 128)
    taken = columns_ref[...].reshape(1024, 128)
    low, high = by_core(core_ref[0], kept, taken)
    hidden = lax.dot_general(
        tower, jnp.concatenate([low, high], axis=1), contract, preferred_element_type=f32
    )
    spread(out_ref, rms_norm(hidden))


def energy_blocks(points_ref, lists_ref, energy_ref):
    points = points_ref[...].reshape(8 * ROWS, DP)
    ones = split_rows(jnp.ones((1, 8 * ROWS), f32))
    tiles = []
    for k in range(4):
        rows = pl.ds(256 * k, 256)
        scores = lax.dot_general(
            lists_ref[rows, :], points, (((1,), (1,)), ((), ())), preferred_element_type=f32
        )
        block = jnp.exp2(scores * SLOPE - OFFSET).astype(bf16)
        energy_ref[rows, :] = block
        tiles.append(
            to_tile(
                lax.dot_general(ones, block, (((1,), (1,)), ((), ())), preferred_element_type=f32)
            )
        )
    return jnp.concatenate(tiles, axis=0)


def first_kernel(points_ref, lists_ref, energy_ref, column_ref):
    column_ref[...] = energy_blocks(points_ref, lists_ref, energy_ref)


def second_kernel(points_ref, lists_ref, first_ref, energy_ref, column_ref):
    spread(column_ref, first_ref[...] + energy_blocks(points_ref, lists_ref, energy_ref))


def row_kernel(core_ref, parts_ref, own_ref, other_ref, row_ref):
    lhs = split_rows(to_lanes(2.0 / add_parts(parts_ref)))
    own = to_tile(jnp.dot(lhs, own_ref[...], preferred_element_type=f32))
    other = to_tile(jnp.dot(lhs, other_ref[...], preferred_element_type=f32))
    spread(row_ref, jnp.concatenate(by_core(core_ref[0], own, other), axis=0))


def row_scales(core_ref, rows_ref):
    scale = 1.0 / add_parts(rows_ref)
    return by_core(core_ref[0], scale[:8], scale[8:])


def column_kernel(core_ref, rows_ref, own_ref, other_ref, column_ref):
    own, other = row_scales(core_ref, rows_ref)
    rows = column_rows(own, own_ref[...]) + column_rows(other, other_ref[...])
    spread(column_ref, to_tile(rows))


def down_lanes(row):
    return jnp.transpose(jnp.broadcast_to(row, (128, 128)))


def scaled_points(scale, points_ref):
    blocks = []
    for k in range(8):
        factor = down_lanes(scale[k : k + 1])
        block = points_ref[k].astype(f32) * jnp.concatenate([factor, factor], axis=1)
        blocks.append(block.astype(bf16))
    return jnp.concatenate(blocks, axis=0)


def update_kernel(
    core_ref, rows_ref, columns_ref, own_ref, other_ref, own_points, other_points, out_ref, log_ref
):
    own, other = row_scales(core_ref, rows_ref)
    log_ref[...] = jnp.log(own)
    col_scale = 2.0 / add_parts(columns_ref)
    own = scaled_points(own, own_points)
    other = scaled_points(other, other_points)
    for k in range(4):
        rows = pl.ds(256 * k, 256)
        sums = jnp.dot(own_ref[rows, :], own, preferred_element_type=f32)
        sums += jnp.dot(other_ref[rows, :], other, preferred_element_type=f32)
        for n in range(2):
            factor = down_lanes(col_scale[2 * k + n : 2 * k + n + 1])
            block = sums[128 * n : 128 * (n + 1)] * jnp.concatenate([factor, factor], axis=1)
            start = 4 * k + 2 * n
            out_ref[start : start + 2] = block.astype(bf16).reshape(2, 64, DP)


def finish_kernel(parts_ref, out_ref):
    out_ref[...] = rms_norm(add_parts(parts_ref))


def shape(dims, dtype):
    return jax.ShapeDtypeStruct(dims, dtype)


def on_device(tower_out, projection, centroids):
    half = lax.axis_index("yh")
    core = lax.axis_index("c")
    core_index = core.reshape(1)
    pairs = centroids.reshape(8, 2, 64, DP)
    kept = jnp.where(core == 0, pairs[:, 0], pairs[:, 1]).reshape(512, DP)
    taken = lax.ppermute(kept, "yh", SWAP)
    message = pl.pallas_call(
        pack_kernel,
        out_shape=shape((16, 128, 128), bf16),
        in_specs=[SCALAR] + [pl.BlockSpec(memory_space=pltpu.HBM)] * 2,
        out_specs=pl.BlockSpec(memory_space=VMEM),
        scratch_shapes=[
            VMEM((64, 2048), bf16),
            VMEM((64, 128), bf16),
            pltpu.SemaphoreType.DMA((2,)),
        ],
        compiler_params=LIMIT,
        name="pack",
    )(core_index, far(tower_out.T), far(projection))
    parts = lax.all_to_all(message, ("z", "yh"), 0, 0)
    parts, taken = lax.optimization_barrier((parts, taken))
    taken_columns = lax.ppermute(parts[:, 64:], "c", SWAP)
    unit_lists = call(lists_kernel, shape((1024, DP), bf16), "lists", 1, 2, cost=COST)(
        half.reshape(1), kept, taken
    )
    taken_columns, unit_lists = lax.optimization_barrier((taken_columns, unit_lists))
    gathered = call(hidden_kernel, shape((8, ROWS, DP), bf16), "hidden", 1, 2)(
        core_index, parts, taken_columns
    )
    points = lax.all_to_all(gathered, "z", 0, 0)
    other_points = lax.ppermute(points, "c", SWAP)

    energy_shape = VMEM((1024, 1024), bf16)
    own_energy, first = call(
        first_kernel, (energy_shape, shape((8, 128), f32)), "first_energy", 0, 2, cost=COST
    )(points, unit_lists)
    other_energy, columns = call(
        second_kernel, (energy_shape, shape((16, 8, 128), f32)), "second_energy", 0, 3, cost=COST
    )(other_points, unit_lists, first)

    for sweep in range(ITERS):
        last = sweep == ITERS - 1
        columns = lax.all_to_all(columns, CHIPS, 0, 0)
        rows = call(row_kernel, shape((16, 16, 128), f32 if last else bf16), "row_sums", 1, 3)(
            core_index, columns, stay(own_energy), stay(other_energy)
        )
        rows = lax.all_to_all(rows, LISTS, 0, 0)
        if not last:
            columns = call(column_kernel, shape((16, 8, 128), f32), "column_sums", 1, 3)(
                core_index, rows, stay(own_energy), stay(other_energy)
            )

    sums, row_log = call(
        update_kernel, (shape((16, 64, DP), bf16), shape((8, 128), f32)), "update", 1, 6
    )(core_index, rows, columns, stay(own_energy), stay(other_energy), points, other_points)
    owned = lax.all_to_all(sums, CHIPS, 0, 0)
    refreshed = call(finish_kernel, shape((64, DP), f32), "finish", 0, 1)(owned)

    taken_log = lax.ppermute(row_log, "yh", SWAP)
    low_log = jnp.where(half == 0, row_log, taken_log)
    high_log = jnp.where(half == 0, taken_log, row_log)
    row_log = jnp.stack([low_log, high_log], axis=1).reshape(16 * ROWS)
    return (refreshed, row_log)


def solution(mesh):
    fine = Mesh(mesh.devices.reshape(4, 2, 2, 8, 2), ("x", "yl", "c", "z", "yh"))
    pts, lst = ("x", "yl", "c"), ("z", "yh")
    return jax.shard_map(
        on_device,
        mesh=fine,
        in_specs=(P(pts, lst), P(lst, None), P(lst, None)),
        out_specs=(P(lst + pts, None), P(pts)),
        check_vma=False,
    )
```

time: 197 us -> 151 us (0.77)
  other arithmetic: 29.2 us -> 0.04 us
  waiting for transfers between devices: 46.6 us -> 23.9 us
  blocking collectives: 74.5 us -> 87.2 us
  Pallas kernels: 0 us -> 12.6 us
  matrix products: 10.7 us -> 0 us
  local copies, waits for them, and re-layouts: 9.46 us -> 0.63 us
    all_to_all x3 -> x2, waiting for transfers between devices: 37 us -> 13.7 us  [the longest x1 7.56 us: on_device(): parts = lax.all_to_all(message, ('z', 'yh'), 0, 0)]
    reduce_sum x16 -> x0, other arithmetic: 20.9 us -> none  [the longest x3 12.1 us: on_device(): row_local = jnp.sum(energy(normed, unit_lists) * col_scale[None, :], axis=1)]
    all_to_all x6 -> x7, blocking collectives: 74.5 us -> 87.2 us  [the longest x3 37.1 us: on_device(): rows = lax.all_to_all(rows, LISTS, 0, 0)]
    pallas_call x0 -> x12, Pallas kernels: none -> 12.6 us  [the longest x2 2.4 us: on_device(): call(column_kernel, shape((16, 8, 128), f32), 'column_sums', 1, 3)]
    dot_general x4 -> x0, matrix products: 10.7 us -> none  [the longest x1 5.01 us: energy(): lax.dot_general(points, unit_lists, (((1,), (1,)), ((), ())), preferred_e...]
    convert_element_type x3 -> x0, other arithmetic: 7.22 us -> none  [the longest x1 6.11 us: on_device(): weights.astype(bf16)]
    convert_element_type x1 -> x0, local copies, waits for them, and re-layouts: 6.4 us -> none  [on_device(): weights.astype(bf16)]
    ppermute x1, starting transfers between devices: 0.78 us -> 2.8 us  [on_device(): taken_log = lax.ppermute(row_log, 'yh', SWAP)]
  transfers between devices with their start and end apart: 8 -> 6, of which waited for: 6 -> 6; matrix products, arithmetic and copies ran while one was open for 2% -> 0% of each run, Pallas kernels for 0% -> 1%
where the time goes in v4:
time: 151 us; the launch traced here: 150 us
  blocking collectives  87.2 us (58%)
  starting transfers between devices  25.4 us (17%)
  waiting for transfers between devices  23.9 us (16%)
  Pallas kernels  12.6 us (8%)
    all_to_all x3, blocking collectives, on_device(): rows = lax.all_to_all(rows, LISTS, 0, 0)  37.1 us
    all_to_all x3, blocking collectives, on_device(): columns = lax.all_to_all(columns, CHIPS, 0, 0)  30.9 us
    all_to_all x1, blocking collectives, on_device(): points = lax.all_to_all(gathered, 'z', 0, 0)  19.2 us
    all_to_all x1, starting transfers between devices, on_device(): parts = lax.all_to_all(message, ('z', 'yh'), 0, 0)  11.8 us
    all_to_all x1, waiting for transfers between devices, on_device(): parts = lax.all_to_all(message, ('z', 'yh'), 0, 0)  7.56 us
    ppermute x1, waiting for transfers between devices, on_device(): taken = lax.ppermute(kept, 'yh', SWAP)  6.57 us
    all_to_all x1, waiting for transfers between devices, on_device(): owned = lax.all_to_all(sums, CHIPS, 0, 0)  6.13 us
    all_to_all x1, starting transfers between devices, on_device(): owned = lax.all_to_all(sums, CHIPS, 0, 0)  3.57 us
  transfers between devices with their start and end apart: 6, of which 6 were waited for; matrix products, arithmetic and copies ran while one was open for 0% of the time, Pallas kernels for 1%

profile of v4, /device:TPU:1, one launch (start us, length us, event | category | flops | bytes accessed | tf_op | source)
XLA Modules:
  0.0 150.5 jit_solution(776553596483376793)
XLA Ops:
  0.6 0.0 copy-start
  0.6 1.9 %pack.1 = bf16[16,128,128]{2,1,0:T(8,128)(2,1)} custom-call(s32[1]{0:T(128)} %bitcast.core_ref, bf16[64,2048]{1,0:T(8,128)(2,1)} %bitcast.21, bf16[64,256]{1,0:T(8,128)(2,1)} %projection_ref.1), custom_call_target="tpu_custom_call" | custom-call | tf_op jit(solution)/shard_map/pack/pallas_call | solution.py:227
  2.5 11.8 %all-to-all-start = ((bf16[16,128,128]{2,1,0:T(8,128)(2,1)}), bf16[16,128,128]{2,1,0:T(8,128)(2,1)S(1)}, u32[]{:S(2)}, u32[]{:S(2)}) async-start(bf16[16,128,128]{2,1,0:T(8,128)(2,1)} %pack.1), calls=%async_computation | async-start | bytes 1048576 | tf_op jit(solution)/shard_map/all_to_all | solution.py:240
  14.3 0.0 copy-done
  14.3 2.9 %collective-permute-start = (bf16[512,256]{1,0:T(8,128)(2,1)S(1)}, bf16[512,256]{1,0:T(8,128)(2,1)S(1)}, u32[]{:S(2)}, u32[]{:S(2)}) collective-permute-start(bf16[512,256]{1,0:T(8,128)(2,1)S(1)} %bitcast.18), channel_id=1, source_target_pairs={{0,1},{1,0},{2,3},{3,2},{4,5},{5,4},{6,7},{7,6},{8,9},{9,8},{10,11... | collective-permute-start | bytes 786440 | tf_op jit(solution)/shard_map/ppermute | solution.py:226
  17.3 6.6 %collective-permute-done.taken_ref = bf16[512,256]{1,0:T(8,128)(2,1)S(1)} collective-permute-done((bf16[512,256]{1,0:T(8,128)(2,1)S(1)}, bf16[512,256]{1,0:T(8,128)(2,1)S(1)}, u32[]{:S(2)}, u32[]{:S(2)}) %collective-permute-start) | collective-permute-done | bytes 262176 | tf_op jit(solution)/shard_map/ppermute | solution.py:226
  23.9 7.6 %all-to-all-done.parts_ref = bf16[16,128,128]{2,1,0:T(8,128)(2,1)S(1)} async-done(((bf16[16,128,128]{2,1,0:T(8,128)(2,1)}), bf16[16,128,128]{2,1,0:T(8,128)(2,1)S(1)}, u32[]{:S(2)}, u32[]{:S(2)}) %all-to-all-start) | async-done | bytes 524320 | tf_op jit(solution)/shard_map/all_to_all | solution.py:240
  31.5 2.6 %collective-permute-start.1 = (bf16[16,64,128]{2,1,0:T(8,128)(2,1)S(1)}, bf16[16,64,128]{2,1,0:T(8,128)(2,1)S(1)}, u32[]{:S(2)}, u32[]{:S(2)}) collective-permute-start(bf16[16,64,128]{2,1,0:T(8,128)(2,1)S(1)} %slice.11), channel_id=1, source_target_pairs={{0,16},{16,0},{1,17},{17,1},{2,18},{18,2},{3,19},{19,3},{4,20},{20... | collective-permute-start | bytes 786440 | tf_op jit(solution)/shard_map/ppermute | solution.py:242
  34.0 0.2 lists.1.lists_ref
  34.2 0.9 collective-permute-done.1.columns_ref
  35.2 0.4 hidden.1
  35.6 19.2 %all_to_all.45.points_ref.own_points = bf16[8,128,256]{2,1,0:T(8,128)(2,1)S(1)} all-to-all(bf16[8,128,256]{2,1,0:T(8,128)(2,1)S(1)} %hidden.1), channel_id=1, replica_groups=mesh['x'=4,'yl'=2,'c'=2,'z'=8,'yh'=2] {'z'}, dimensions={0} | all-to-all | bytes 1048576 | tf_op jit(solution)/shard_map/all_to_all | solution.py:250
  54.8 1.7 %collective-permute-start.2 = (bf16[8,128,256]{2,1,0:T(8,128)(2,1)S(1)}, bf16[8,128,256]{2,1,0:T(8,128)(2,1)S(1)}, u32[]{:S(2)}, u32[]{:S(2)}) collective-permute-start(bf16[8,128,256]{2,1,0:T(8,128)(2,1)S(1)} %all_to_all.45.points_ref.own_points), channel_id=1, source_target_pairs={{0,16},{16,0},{1,17},{17,1},{2,18},{18,2},{3,19},{19,3},{4,20},{20... | collective-permute-start | bytes 1572872 | tf_op jit(solution)/shard_map/ppermute | solution.py:251
  56.5 1.3 first_energy.1
  57.9 0.2 collective-permute-done.2.points_ref.other_points
  58.0 1.4 second_energy.1
  59.4 12.0 %all_to_all.46.parts_ref = f32[16,8,128]{2,1,0:T(8,128)S(1)} all-to-all(f32[16,8,128]{2,1,0:T(8,128)S(1)} %get-tuple-element.17), channel_id=1, replica_groups=mesh['x'=4,'yl'=2,'c'=2,'z'=8,'yh'=2] {'yh','x','yl'}, dimensions={0} | all-to-all | bytes 131072 | tf_op jit(solution)/shard_map/all_to_all | solution.py:263
  71.4 0.7 row_sums.3
  72.1 12.0 %all_to_all.47.rows_ref = bf16[16,16,128]{2,1,0:T(8,128)(2,1)S(1)} all-to-all(bf16[16,16,128]{2,1,0:T(8,128)(2,1)S(1)} %row_sums.3), channel_id=1, replica_groups=mesh['x'=4,'yl'=2,'c'=2,'z'=8,'yh'=2] {'z','c'}, dimensions={0} | all-to-all | bytes 131072 | tf_op jit(solution)/shard_map/all_to_all | solution.py:267
  84.1 1.2 column_sums.2
  85.4 9.5 %all_to_all.48.parts_ref = f32[16,8,128]{2,1,0:T(8,128)S(1)} all-to-all(f32[16,8,128]{2,1,0:T(8,128)S(1)} %column_sums.2), channel_id=1, replica_groups=mesh['x'=4,'yl'=2,'c'=2,'z'=8,'yh'=2] {'yh','x','yl'}, dimensions={0} | all-to-all | bytes 131072 | tf_op jit(solution)/shard_map/all_to_all | solution.py:263
  94.8 0.7 row_sums.4
  95.5 11.8 %all_to_all.49.rows_ref = bf16[16,16,128]{2,1,0:T(8,128)(2,1)S(1)} all-to-all(bf16[16,16,128]{2,1,0:T(8,128)(2,1)S(1)} %row_sums.4), channel_id=1, replica_groups=mesh['x'=4,'yl'=2,'c'=2,'z'=8,'yh'=2] {'z','c'}, dimensions={0} | all-to-all | bytes 131072 | tf_op jit(solution)/shard_map/all_to_all | solution.py:267
  107.3 1.2 column_sums.3
  108.5 9.5 %all_to_all.50.parts_ref.columns_ref = f32[16,8,128]{2,1,0:T(8,128)S(1)} all-to-all(f32[16,8,128]{2,1,0:T(8,128)S(1)} %column_sums.3), channel_id=1, replica_groups=mesh['x'=4,'yl'=2,'c'=2,'z'=8,'yh'=2] {'yh','x','yl'}, dimensions={0} | all-to-all | bytes 131072 | tf_op jit(solution)/shard_map/all_to_all | solution.py:263
  118.0 0.7 row_sums.5
  118.7 13.2 %all_to_all.51.rows_ref = f32[16,16,128]{2,1,0:T(8,128)S(1)} all-to-all(f32[16,16,128]{2,1,0:T(8,128)S(1)} %row_sums.5), channel_id=1, replica_groups=mesh['x'=4,'yl'=2,'c'=2,'z'=8,'yh'=2] {'z','c'}, dimensions={0} | all-to-all | bytes 262144 | tf_op jit(solution)/shard_map/all_to_all | solution.py:267
  131.9 2.2 %update.1 = (bf16[16,64,256]{2,1,0:T(8,128)(2,1)}, f32[8,128]{1,0:T(8,128)S(1)}) custom-call(s32[1]{0:T(128)} %bitcast.core_ref, f32[16,16,128]{2,1,0:T(8,128)S(1)} %all_to_all.51.rows_ref, f32[16,8,128]{2,1,0:T(8,128)S(1)} %all_to_all.50.parts_ref.columns_ref, bf16[1024,1024]{1,0:T(8,128)(2,1)S(1)} %get-tuple-element.18.own_ref, ...), custom_call_target="tpu_custom_call" | custom-call | tf_op jit(solution)/shard_map/update/pallas_call | solution.py:273
  134.1 3.6 %all-to-all-start.8 = ((bf16[16,64,256]{2,1,0:T(8,128)(2,1)}), bf16[16,64,256]{2,1,0:T(8,128)(2,1)S(1)}, u32[]{:S(2)}, u32[]{:S(2)}) async-start(bf16[16,64,256]{2,1,0:T(8,128)(2,1)} %get-tuple-element.20), calls=%async_computation.8 | async-start | bytes 1048576 | tf_op jit(solution)/shard_map/all_to_all | solution.py:276
  137.7 2.8 %collective-permute-start.3 = (f32[8,128]{1,0:T(8,128)S(1)}, f32[8,128]{1,0:T(8,128)S(1)}, u32[]{:S(2)}, u32[]{:S(2)}) collective-permute-start(f32[8,128]{1,0:T(8,128)S(1)} %get-tuple-element.21), channel_id=1, source_target_pairs={{0,1},{1,0},{2,3},{3,2},{4,5},{5,4},{6,7},{7,6},{8,9},{9,8},{10,11... | collective-permute-start | bytes 12296 | tf_op jit(solution)/shard_map/ppermute | solution.py:279
  140.5 2.5 %collective-permute-done.3 = f32[8,128]{1,0:T(8,128)S(1)} collective-permute-done((f32[8,128]{1,0:T(8,128)S(1)}, f32[8,128]{1,0:T(8,128)S(1)}, u32[]{:S(2)}, u32[]{:S(2)}) %collective-permute-start.3) | collective-permute-done | bytes 4128 | tf_op jit(solution)/shard_map/ppermute | solution.py:279
  142.9 0.6 copy.9
  143.6 6.1 %all-to-all-done.8.parts_ref = bf16[16,64,256]{2,1,0:T(8,128)(2,1)S(1)} async-done(((bf16[16,64,256]{2,1,0:T(8,128)(2,1)}), bf16[16,64,256]{2,1,0:T(8,128)(2,1)S(1)}, u32[]{:S(2)}, u32[]{:S(2)}) %all-to-all-start.8) | async-done | bytes 524320 | tf_op jit(solution)/shard_map/all_to_all | solution.py:276
  149.7 0.8 finish.1
  (4 shorter events, 0.1 us)
Async XLA Ops:
  0.6 13.7 %copy-start = (bf16[1024,256]{1,0:T(8,128)(2,1)S(1)}, bf16[1024,256]{1,0:T(8,128)(2,1)}, u32[]{:S(2)}) copy-start(bf16[1024,256]{1,0:T(8,128)(2,1)} %param.5) | copy-start | bytes 1572868
  2.5 28.9 %all-to-all-start = ((bf16[16,128,128]{2,1,0:T(8,128)(2,1)}), bf16[16,128,128]{2,1,0:T(8,128)(2,1)S(1)}, u32[]{:S(2)}, u32[]{:S(2)}) async-start(bf16[16,128,128]{2,1,0:T(8,128)(2,1)} %pack.1), calls=%async_computation | async-start | bytes 1048576 | tf_op jit(solution)/shard_map/all_to_all | solution.py:240
  14.3 9.5 %collective-permute-start = (bf16[512,256]{1,0:T(8,128)(2,1)S(1)}, bf16[512,256]{1,0:T(8,128)(2,1)S(1)}, u32[]{:S(2)}, u32[]{:S(2)}) collective-permute-start(bf16[512,256]{1,0:T(8,128)(2,1)S(1)} %bitcast.18), channel_id=1, source_target_pairs={{0,1},{1,0},{2,3},{3,2},{4,5},{5,4},{6,7},{7,6},{8,9},{9,8},{10,11... | collective-permute-start | bytes 786440 | tf_op jit(solution)/shard_map/ppermute | solution.py:226
  31.5 3.7 %collective-permute-start.1 = (bf16[16,64,128]{2,1,0:T(8,128)(2,1)S(1)}, bf16[16,64,128]{2,1,0:T(8,128)(2,1)S(1)}, u32[]{:S(2)}, u32[]{:S(2)}) collective-permute-start(bf16[16,64,128]{2,1,0:T(8,128)(2,1)S(1)} %slice.11), channel_id=1, source_target_pairs={{0,16},{16,0},{1,17},{17,1},{2,18},{18,2},{3,19},{19,3},{4,20},{20... | collective-permute-start | bytes 786440 | tf_op jit(solution)/shard_map/ppermute | solution.py:242
  54.8 3.3 %collective-permute-start.2 = (bf16[8,128,256]{2,1,0:T(8,128)(2,1)S(1)}, bf16[8,128,256]{2,1,0:T(8,128)(2,1)S(1)}, u32[]{:S(2)}, u32[]{:S(2)}) collective-permute-start(bf16[8,128,256]{2,1,0:T(8,128)(2,1)S(1)} %all_to_all.45.points_ref.own_points), channel_id=1, source_target_pairs={{0,16},{16,0},{1,17},{17,1},{2,18},{18,2},{3,19},{19,3},{4,20},{20... | collective-permute-start | bytes 1572872 | tf_op jit(solution)/shard_map/ppermute | solution.py:251
  134.1 15.6 %all-to-all-start.8 = ((bf16[16,64,256]{2,1,0:T(8,128)(2,1)}), bf16[16,64,256]{2,1,0:T(8,128)(2,1)S(1)}, u32[]{:S(2)}, u32[]{:S(2)}) async-start(bf16[16,64,256]{2,1,0:T(8,128)(2,1)} %get-tuple-element.20), calls=%async_computation.8 | async-start | bytes 1048576 | tf_op jit(solution)/shard_map/all_to_all | solution.py:276
  137.7 5.3 %collective-permute-start.3 = (f32[8,128]{1,0:T(8,128)S(1)}, f32[8,128]{1,0:T(8,128)S(1)}, u32[]{:S(2)}, u32[]{:S(2)}) collective-permute-start(f32[8,128]{1,0:T(8,128)S(1)} %get-tuple-element.21), channel_id=1, source_target_pairs={{0,1},{1,0},{2,3},{3,2},{4,5},{5,4},{6,7},{7,6},{8,9},{9,8},{10,11... | collective-permute-start | bytes 12296 | tf_op jit(solution)/shard_map/ppermute | solution.py:279

commit v5 on v4

--- a/solution.py
+++ b/solution.py
@@ -159,15 +159,24 @@
     spread(column_ref, first_ref[...] + energy_blocks(points_ref, lists_ref, energy_ref))
 
 
-def row_kernel(core_ref, parts_ref, own_ref, other_ref, row_ref):
+def row_tile(core_ref, parts_ref, own_ref, other_ref):
     lhs = split_rows(to_lanes(2.0 / add_parts(parts_ref)))
     own = to_tile(jnp.dot(lhs, own_ref[...], preferred_element_type=f32))
     other = to_tile(jnp.dot(lhs, other_ref[...], preferred_element_type=f32))
-    spread(row_ref, jnp.concatenate(by_core(core_ref[0], own, other), axis=0))
-
-
-def row_scales(core_ref, rows_ref):
-    scale = 1.0 / add_parts(rows_ref)
+    return jnp.concatenate(by_core(core_ref[0], own, other), axis=0)
+
+
+def row_kernel(core_ref, parts_ref, own_ref, other_ref, row_ref):
+    spread(row_ref, row_tile(core_ref, parts_ref, own_ref, other_ref))
+
+
+def change_kernel(core_ref, parts_ref, own_ref, other_ref, sent_ref, row_ref):
+    tile = row_tile(core_ref, parts_ref, own_ref, other_ref)
+    spread(row_ref, tile - sent_ref[0].astype(f32))
+
+
+def row_scales(core_ref, *rows):
+    scale = 1.0 / sum(add_parts(rows_ref) for rows_ref in rows)
     return by_core(core_ref[0], scale[:8], scale[8:])
 
 
@@ -191,9 +200,18 @@
 
 
 def update_kernel(
-    core_ref, rows_ref, columns_ref, own_ref, other_ref, own_points, other_points, out_ref, log_ref
+    core_ref,
+    rows_ref,
+    change_ref,
+    columns_ref,
+    own_ref,
+    other_ref,
+    own_points,
+    other_points,
+    out_ref,
+    log_ref,
 ):
-    own, other = row_scales(core_ref, rows_ref)
+    own, other = row_scales(core_ref, rows_ref, change_ref)
     log_ref[...] = jnp.log(own)
     col_scale = 2.0 / add_parts(columns_ref)
     own = scaled_points(own, own_points)
@@ -258,21 +276,24 @@
         second_kernel, (energy_shape, shape((16, 8, 128), f32)), "second_energy", 0, 3, cost=COST
     )(other_points, unit_lists, first)
 
-    for sweep in range(ITERS):
-        last = sweep == ITERS - 1
+    sent_shape = shape((16, 16, 128), bf16)
+    energies = (stay(own_energy), stay(other_energy))
+    for sweep in range(ITERS - 1):
         columns = lax.all_to_all(columns, CHIPS, 0, 0)
-        rows = call(row_kernel, shape((16, 16, 128), f32 if last else bf16), "row_sums", 1, 3)(
-            core_index, columns, stay(own_energy), stay(other_energy)
+        sent = call(row_kernel, sent_shape, "row_sums", 1, 3)(core_index, columns, *energies)
+        rows = lax.all_to_all(sent, LISTS, 0, 0)
+        columns = call(column_kernel, shape((16, 8, 128), f32), "column_sums", 1, 3)(
+            core_index, rows, *energies
         )
-        rows = lax.all_to_all(rows, LISTS, 0, 0)
-        if not last:
-            columns = call(column_kernel, shape((16, 8, 128), f32), "column_sums", 1, 3)(
-                core_index, rows, stay(own_energy), stay(other_energy)
-            )
+    columns = lax.all_to_all(columns, CHIPS, 0, 0)
+    change = call(change_kernel, sent_shape, "row_change", 1, 4)(
+        core_index, columns, *energies, sent
+    )
+    change = lax.all_to_all(change, LISTS, 0, 0)
 
     sums, row_log = call(
-        update_kernel, (shape((16, 64, DP), bf16), shape((8, 128), f32)), "update", 1, 6
-    )(core_index, rows, columns, stay(own_energy), stay(other_energy), points, other_points)
+        update_kernel, (shape((16, 64, DP), bf16), shape((8, 128), f32)), "update", 1, 7
+    )(core_index, rows, change, columns, *energies, points, other_points)
     owned = lax.all_to_all(sums, CHIPS, 0, 0)
     refreshed = call(finish_kernel, shape((64, DP), f32), "finish", 0, 1)(owned)
 

time: 151 us -> 149 us (0.987)
  no operation moved by 1% of the time
where the time goes in v5:
time: 149 us; the launch traced here: 148 us
  blocking collectives  85.8 us (58%)
  starting transfers between devices  25.4 us (17%)
  waiting for transfers between devices  23.2 us (16%)
  Pallas kernels  12.6 us (8%)
    all_to_all x3, blocking collectives, on_device(): columns = lax.all_to_all(columns, CHIPS, 0, 0)  30.9 us
    all_to_all x2, blocking collectives, on_device(): rows = lax.all_to_all(sent, LISTS, 0, 0)  23.9 us
    all_to_all x1, blocking collectives, on_device(): points = lax.all_to_all(gathered, 'z', 0, 0)  19.2 us
    all_to_all x1, blocking collectives, on_device(): change = lax.all_to_all(change, LISTS, 0, 0)  11.8 us
    all_to_all x1, starting transfers between devices, on_device(): parts = lax.all_to_all(message, ('z', 'yh'), 0, 0)  11.8 us
    all_to_all x1, waiting for transfers between devices, on_device(): parts = lax.all_to_all(message, ('z', 'yh'), 0, 0)  7.56 us
    ppermute x1, waiting for transfers between devices, on_device(): taken = lax.ppermute(kept, 'yh', SWAP)  6.57 us
    all_to_all x1, waiting for transfers between devices, on_device(): owned = lax.all_to_all(sums, CHIPS, 0, 0)  5.54 us
  transfers between devices with their start and end apart: 6, of which 6 were waited for; matrix products, arithmetic and copies ran while one was open for 0% of the time, Pallas kernels for 1%

profile of v5, /device:TPU:1, one launch (start us, length us, event | category | flops | bytes accessed | tf_op | source)
XLA Modules:
  0.0 148.4 jit_solution(13399225184725016703)
XLA Ops:
  0.6 0.0 copy-start
  0.6 1.9 %pack.1 = bf16[16,128,128]{2,1,0:T(8,128)(2,1)} custom-call(s32[1]{0:T(128)} %bitcast.core_ref, bf16[64,2048]{1,0:T(8,128)(2,1)} %bitcast.21, bf16[64,256]{1,0:T(8,128)(2,1)} %projection_ref.1), custom_call_target="tpu_custom_call" | custom-call | tf_op jit(solution)/shard_map/pack/pallas_call | solution.py:245
  2.5 11.8 %all-to-all-start = ((bf16[16,128,128]{2,1,0:T(8,128)(2,1)}), bf16[16,128,128]{2,1,0:T(8,128)(2,1)S(1)}, u32[]{:S(2)}, u32[]{:S(2)}) async-start(bf16[16,128,128]{2,1,0:T(8,128)(2,1)} %pack.1), calls=%async_computation | async-start | bytes 1048576 | tf_op jit(solution)/shard_map/all_to_all | solution.py:258
  14.3 0.0 copy-done
  14.3 2.9 %collective-permute-start = (bf16[512,256]{1,0:T(8,128)(2,1)S(1)}, bf16[512,256]{1,0:T(8,128)(2,1)S(1)}, u32[]{:S(2)}, u32[]{:S(2)}) collective-permute-start(bf16[512,256]{1,0:T(8,128)(2,1)S(1)} %bitcast.18), channel_id=1, source_target_pairs={{0,1},{1,0},{2,3},{3,2},{4,5},{5,4},{6,7},{7,6},{8,9},{9,8},{10,11... | collective-permute-start | bytes 786440 | tf_op jit(solution)/shard_map/ppermute | solution.py:244
  17.3 6.6 %collective-permute-done.taken_ref = bf16[512,256]{1,0:T(8,128)(2,1)S(1)} collective-permute-done((bf16[512,256]{1,0:T(8,128)(2,1)S(1)}, bf16[512,256]{1,0:T(8,128)(2,1)S(1)}, u32[]{:S(2)}, u32[]{:S(2)}) %collective-permute-start) | collective-permute-done | bytes 262176 | tf_op jit(solution)/shard_map/ppermute | solution.py:244
  23.9 7.6 %all-to-all-done.parts_ref = bf16[16,128,128]{2,1,0:T(8,128)(2,1)S(1)} async-done(((bf16[16,128,128]{2,1,0:T(8,128)(2,1)}), bf16[16,128,128]{2,1,0:T(8,128)(2,1)S(1)}, u32[]{:S(2)}, u32[]{:S(2)}) %all-to-all-start) | async-done | bytes 524320 | tf_op jit(solution)/shard_map/all_to_all | solution.py:258
  31.5 2.6 %collective-permute-start.1 = (bf16[16,64,128]{2,1,0:T(8,128)(2,1)S(1)}, bf16[16,64,128]{2,1,0:T(8,128)(2,1)S(1)}, u32[]{:S(2)}, u32[]{:S(2)}) collective-permute-start(bf16[16,64,128]{2,1,0:T(8,128)(2,1)S(1)} %slice.11), channel_id=1, source_target_pairs={{0,16},{16,0},{1,17},{17,1},{2,18},{18,2},{3,19},{19,3},{4,20},{20... | collective-permute-start | bytes 786440 | tf_op jit(solution)/shard_map/ppermute | solution.py:260
  34.0 0.2 lists.1.lists_ref
  34.2 0.9 collective-permute-done.1.columns_ref
  35.2 0.4 hidden.1
  35.6 19.2 %all_to_all.45.points_ref.own_points = bf16[8,128,256]{2,1,0:T(8,128)(2,1)S(1)} all-to-all(bf16[8,128,256]{2,1,0:T(8,128)(2,1)S(1)} %hidden.1), channel_id=1, replica_groups=mesh['x'=4,'yl'=2,'c'=2,'z'=8,'yh'=2] {'z'}, dimensions={0} | all-to-all | bytes 1048576 | tf_op jit(solution)/shard_map/all_to_all | solution.py:268
  54.8 1.7 %collective-permute-start.2 = (bf16[8,128,256]{2,1,0:T(8,128)(2,1)S(1)}, bf16[8,128,256]{2,1,0:T(8,128)(2,1)S(1)}, u32[]{:S(2)}, u32[]{:S(2)}) collective-permute-start(bf16[8,128,256]{2,1,0:T(8,128)(2,1)S(1)} %all_to_all.45.points_ref.own_points), channel_id=1, source_target_pairs={{0,16},{16,0},{1,17},{17,1},{2,18},{18,2},{3,19},{19,3},{4,20},{20... | collective-permute-start | bytes 1572872 | tf_op jit(solution)/shard_map/ppermute | solution.py:269
  56.5 1.3 first_energy.1
  57.9 0.2 collective-permute-done.2.points_ref.other_points
  58.0 1.4 second_energy.1
  59.4 12.0 %all_to_all.46.parts_ref = f32[16,8,128]{2,1,0:T(8,128)S(1)} all-to-all(f32[16,8,128]{2,1,0:T(8,128)S(1)} %get-tuple-element.17), channel_id=1, replica_groups=mesh['x'=4,'yl'=2,'c'=2,'z'=8,'yh'=2] {'yh','x','yl'}, dimensions={0} | all-to-all | bytes 131072 | tf_op jit(solution)/shard_map/all_to_all | solution.py:282
  71.4 0.7 row_sums.2
  72.1 12.0 %all_to_all.47.rows_ref = bf16[16,16,128]{2,1,0:T(8,128)(2,1)S(1)} all-to-all(bf16[16,16,128]{2,1,0:T(8,128)(2,1)S(1)} %row_sums.2), channel_id=1, replica_groups=mesh['x'=4,'yl'=2,'c'=2,'z'=8,'yh'=2] {'z','c'}, dimensions={0} | all-to-all | bytes 131072 | tf_op jit(solution)/shard_map/all_to_all | solution.py:284
  84.1 1.2 column_sums.2
  85.4 9.5 %all_to_all.48.parts_ref = f32[16,8,128]{2,1,0:T(8,128)S(1)} all-to-all(f32[16,8,128]{2,1,0:T(8,128)S(1)} %column_sums.2), channel_id=1, replica_groups=mesh['x'=4,'yl'=2,'c'=2,'z'=8,'yh'=2] {'yh','x','yl'}, dimensions={0} | all-to-all | bytes 131072 | tf_op jit(solution)/shard_map/all_to_all | solution.py:282
  94.8 0.7 row_sums.3.sent_ref
  95.5 11.8 %all_to_all.49.rows_ref = bf16[16,16,128]{2,1,0:T(8,128)(2,1)S(1)} all-to-all(bf16[16,16,128]{2,1,0:T(8,128)(2,1)S(1)} %row_sums.3.sent_ref), channel_id=1, replica_groups=mesh['x'=4,'yl'=2,'c'=2,'z'=8,'yh'=2] {'z','c'}, dimensions={0} | all-to-all | bytes 131072 | tf_op jit(solution)/shard_map/all_to_all | solution.py:284
  107.3 1.2 column_sums.3
  108.5 9.5 %all_to_all.50.parts_ref.columns_ref = f32[16,8,128]{2,1,0:T(8,128)S(1)} all-to-all(f32[16,8,128]{2,1,0:T(8,128)S(1)} %column_sums.3), channel_id=1, replica_groups=mesh['x'=4,'yl'=2,'c'=2,'z'=8,'yh'=2] {'yh','x','yl'}, dimensions={0} | all-to-all | bytes 131072 | tf_op jit(solution)/shard_map/all_to_all | solution.py:288
  118.0 0.7 row_change.1
  118.7 11.8 %all_to_all.51.change_ref = bf16[16,16,128]{2,1,0:T(8,128)(2,1)S(1)} all-to-all(bf16[16,16,128]{2,1,0:T(8,128)(2,1)S(1)} %row_change.1), channel_id=1, replica_groups=mesh['x'=4,'yl'=2,'c'=2,'z'=8,'yh'=2] {'z','c'}, dimensions={0} | all-to-all | bytes 131072 | tf_op jit(solution)/shard_map/all_to_all | solution.py:292
  130.5 2.2 %update.1 = (bf16[16,64,256]{2,1,0:T(8,128)(2,1)}, f32[8,128]{1,0:T(8,128)S(1)}) custom-call(s32[1]{0:T(128)} %bitcast.core_ref, bf16[16,16,128]{2,1,0:T(8,128)(2,1)S(1)} %all_to_all.49.rows_ref, bf16[16,16,128]{2,1,0:T(8,128)(2,1)S(1)} %all_to_all.51.change_ref, f32[16,8,128]{2,1,0:T(8,128)S(1)} %all_to_all.50.parts_ref.columns_ref, ...), custom_call_target="tpu_custom_call" | custom-call | tf_op jit(solution)/shard_map/update/pallas_call | solution.py:294
  132.7 3.6 %all-to-all-start.8 = ((bf16[16,64,256]{2,1,0:T(8,128)(2,1)}), bf16[16,64,256]{2,1,0:T(8,128)(2,1)S(1)}, u32[]{:S(2)}, u32[]{:S(2)}) async-start(bf16[16,64,256]{2,1,0:T(8,128)(2,1)} %get-tuple-element.20), calls=%async_computation.8 | async-start | bytes 1048576 | tf_op jit(solution)/shard_map/all_to_all | solution.py:297
  136.3 2.8 %collective-permute-start.3 = (f32[8,128]{1,0:T(8,128)S(1)}, f32[8,128]{1,0:T(8,128)S(1)}, u32[]{:S(2)}, u32[]{:S(2)}) collective-permute-start(f32[8,128]{1,0:T(8,128)S(1)} %get-tuple-element.21), channel_id=1, source_target_pairs={{0,1},{1,0},{2,3},{3,2},{4,5},{5,4},{6,7},{7,6},{8,9},{9,8},{10,11... | collective-permute-start | bytes 12296 | tf_op jit(solution)/shard_map/ppermute | solution.py:300
  139.1 2.4 %collective-permute-done.3 = f32[8,128]{1,0:T(8,128)S(1)} collective-permute-done((f32[8,128]{1,0:T(8,128)S(1)}, f32[8,128]{1,0:T(8,128)S(1)}, u32[]{:S(2)}, u32[]{:S(2)}) %collective-permute-start.3) | collective-permute-done | bytes 4128 | tf_op jit(solution)/shard_map/ppermute | solution.py:300
  141.5 0.6 copy.9
  142.1 5.5 %all-to-all-done.8.parts_ref = bf16[16,64,256]{2,1,0:T(8,128)(2,1)S(1)} async-done(((bf16[16,64,256]{2,1,0:T(8,128)(2,1)}), bf16[16,64,256]{2,1,0:T(8,128)(2,1)S(1)}, u32[]{:S(2)}, u32[]{:S(2)}) %all-to-all-start.8) | async-done | bytes 524320 | tf_op jit(solution)/shard_map/all_to_all | solution.py:297
  147.6 0.8 finish.1
  (4 shorter events, 0.1 us)
Async XLA Ops:
  0.6 13.7 %copy-start = (bf16[1024,256]{1,0:T(8,128)(2,1)S(1)}, bf16[1024,256]{1,0:T(8,128)(2,1)}, u32[]{:S(2)}) copy-start(bf16[1024,256]{1,0:T(8,128)(2,1)} %param.5) | copy-start | bytes 1572868
  2.5 28.9 %all-to-all-start = ((bf16[16,128,128]{2,1,0:T(8,128)(2,1)}), bf16[16,128,128]{2,1,0:T(8,128)(2,1)S(1)}, u32[]{:S(2)}, u32[]{:S(2)}) async-start(bf16[16,128,128]{2,1,0:T(8,128)(2,1)} %pack.1), calls=%async_computation | async-start | bytes 1048576 | tf_op jit(solution)/shard_map/all_to_all | solution.py:258
  14.3 9.5 %collective-permute-start = (bf16[512,256]{1,0:T(8,128)(2,1)S(1)}, bf16[512,256]{1,0:T(8,128)(2,1)S(1)}, u32[]{:S(2)}, u32[]{:S(2)}) collective-permute-start(bf16[512,256]{1,0:T(8,128)(2,1)S(1)} %bitcast.18), channel_id=1, source_target_pairs={{0,1},{1,0},{2,3},{3,2},{4,5},{5,4},{6,7},{7,6},{8,9},{9,8},{10,11... | collective-permute-start | bytes 786440 | tf_op jit(solution)/shard_map/ppermute | solution.py:244
  31.5 3.7 %collective-permute-start.1 = (bf16[16,64,128]{2,1,0:T(8,128)(2,1)S(1)}, bf16[16,64,128]{2,1,0:T(8,128)(2,1)S(1)}, u32[]{:S(2)}, u32[]{:S(2)}) collective-permute-start(bf16[16,64,128]{2,1,0:T(8,128)(2,1)S(1)} %slice.11), channel_id=1, source_target_pairs={{0,16},{16,0},{1,17},{17,1},{2,18},{18,2},{3,19},{19,3},{4,20},{20... | collective-permute-start | bytes 786440 | tf_op jit(solution)/shard_map/ppermute | solution.py:260
  54.8 3.3 %collective-permute-start.2 = (bf16[8,128,256]{2,1,0:T(8,128)(2,1)S(1)}, bf16[8,128,256]{2,1,0:T(8,128)(2,1)S(1)}, u32[]{:S(2)}, u32[]{:S(2)}) collective-permute-start(bf16[8,128,256]{2,1,0:T(8,128)(2,1)S(1)} %all_to_all.45.points_ref.own_points), channel_id=1, source_target_pairs={{0,16},{16,0},{1,17},{17,1},{2,18},{18,2},{3,19},{19,3},{4,20},{20... | collective-permute-start | bytes 1572872 | tf_op jit(solution)/shard_map/ppermute | solution.py:269
  132.7 14.9 %all-to-all-start.8 = ((bf16[16,64,256]{2,1,0:T(8,128)(2,1)}), bf16[16,64,256]{2,1,0:T(8,128)(2,1)S(1)}, u32[]{:S(2)}, u32[]{:S(2)}) async-start(bf16[16,64,256]{2,1,0:T(8,128)(2,1)} %get-tuple-element.20), calls=%async_computation.8 | async-start | bytes 1048576 | tf_op jit(solution)/shard_map/all_to_all | solution.py:297
  136.3 5.2 %collective-permute-start.3 = (f32[8,128]{1,0:T(8,128)S(1)}, f32[8,128]{1,0:T(8,128)S(1)}, u32[]{:S(2)}, u32[]{:S(2)}) collective-permute-start(f32[8,128]{1,0:T(8,128)S(1)} %get-tuple-element.21), channel_id=1, source_target_pairs={{0,1},{1,0},{2,3},{3,2},{4,5},{5,4},{6,7},{7,6},{8,9},{9,8},{10,11... | collective-permute-start | bytes 12296 | tf_op jit(solution)/shard_map/ppermute | solution.py:300

commit v6 on v5

--- a/solution.py
+++ b/solution.py
@@ -16,7 +16,7 @@
 OFFSET = math.log2(math.e) / temper
 SWAP = [(0, 1), (1, 0)]
 CHIPS = ("yh", "x", "yl")
-LISTS = ("z", "c")
+LISTS = ("c", "z")
 bf16 = jnp.bfloat16
 f32 = jnp.float32
 VMEM = pltpu.VMEM

time: 149 us -> 148 us (level)
  no operation moved by 1% of the time
where the time goes in v6:
time: 148 us; the launch traced here: 147 us
  blocking collectives  85.4 us (58%)
  starting transfers between devices  25.4 us (17%)
  waiting for transfers between devices  22.5 us (15%)
  Pallas kernels  12.6 us (9%)
    all_to_all x3, blocking collectives, on_device(): columns = lax.all_to_all(columns, CHIPS, 0, 0)  31 us
    all_to_all x2, blocking collectives, on_device(): rows = lax.all_to_all(sent, LISTS, 0, 0)  23.3 us
    all_to_all x1, blocking collectives, on_device(): points = lax.all_to_all(gathered, 'z', 0, 0)  19.2 us
    all_to_all x1, blocking collectives, on_device(): change = lax.all_to_all(change, LISTS, 0, 0)  11.9 us
    all_to_all x1, starting transfers between devices, on_device(): parts = lax.all_to_all(message, ('z', 'yh'), 0, 0)  11.8 us
    all_to_all x1, waiting for transfers between devices, on_device(): parts = lax.all_to_all(message, ('z', 'yh'), 0, 0)  7.56 us
    ppermute x1, waiting for transfers between devices, on_device(): taken = lax.ppermute(kept, 'yh', SWAP)  6.57 us
    all_to_all x1, waiting for transfers between devices, on_device(): owned = lax.all_to_all(sums, CHIPS, 0, 0)  5.32 us
  transfers between devices with their start and end apart: 6, of which 6 were waited for; matrix products, arithmetic and copies ran while one was open for 0% of the time, Pallas kernels for 1%

profile of v6, /device:TPU:1, one launch (start us, length us, event | category | flops | bytes accessed | tf_op | source)
XLA Modules:
  0.0 147.3 jit_solution(895167751650196551)
XLA Ops:
  0.6 0.0 copy-start
  0.6 1.9 %pack.1 = bf16[16,128,128]{2,1,0:T(8,128)(2,1)} custom-call(s32[1]{0:T(128)} %bitcast.core_ref, bf16[64,2048]{1,0:T(8,128)(2,1)} %bitcast.21, bf16[64,256]{1,0:T(8,128)(2,1)} %projection_ref.1), custom_call_target="tpu_custom_call" | custom-call | tf_op jit(solution)/shard_map/pack/pallas_call | solution.py:245
  2.5 11.8 %all-to-all-start = ((bf16[16,128,128]{2,1,0:T(8,128)(2,1)}), bf16[16,128,128]{2,1,0:T(8,128)(2,1)S(1)}, u32[]{:S(2)}, u32[]{:S(2)}) async-start(bf16[16,128,128]{2,1,0:T(8,128)(2,1)} %pack.1), calls=%async_computation | async-start | bytes 1048576 | tf_op jit(solution)/shard_map/all_to_all | solution.py:258
  14.3 0.0 copy-done
  14.3 2.9 %collective-permute-start = (bf16[512,256]{1,0:T(8,128)(2,1)S(1)}, bf16[512,256]{1,0:T(8,128)(2,1)S(1)}, u32[]{:S(2)}, u32[]{:S(2)}) collective-permute-start(bf16[512,256]{1,0:T(8,128)(2,1)S(1)} %bitcast.18), channel_id=1, source_target_pairs={{0,1},{1,0},{2,3},{3,2},{4,5},{5,4},{6,7},{7,6},{8,9},{9,8},{10,11... | collective-permute-start | bytes 786440 | tf_op jit(solution)/shard_map/ppermute | solution.py:244
  17.3 6.6 %collective-permute-done.taken_ref = bf16[512,256]{1,0:T(8,128)(2,1)S(1)} collective-permute-done((bf16[512,256]{1,0:T(8,128)(2,1)S(1)}, bf16[512,256]{1,0:T(8,128)(2,1)S(1)}, u32[]{:S(2)}, u32[]{:S(2)}) %collective-permute-start) | collective-permute-done | bytes 262176 | tf_op jit(solution)/shard_map/ppermute | solution.py:244
  23.9 7.6 %all-to-all-done.parts_ref = bf16[16,128,128]{2,1,0:T(8,128)(2,1)S(1)} async-done(((bf16[16,128,128]{2,1,0:T(8,128)(2,1)}), bf16[16,128,128]{2,1,0:T(8,128)(2,1)S(1)}, u32[]{:S(2)}, u32[]{:S(2)}) %all-to-all-start) | async-done | bytes 524320 | tf_op jit(solution)/shard_map/all_to_all | solution.py:258
  31.5 2.6 %collective-permute-start.1 = (bf16[16,64,128]{2,1,0:T(8,128)(2,1)S(1)}, bf16[16,64,128]{2,1,0:T(8,128)(2,1)S(1)}, u32[]{:S(2)}, u32[]{:S(2)}) collective-permute-start(bf16[16,64,128]{2,1,0:T(8,128)(2,1)S(1)} %slice.11), channel_id=1, source_target_pairs={{0,16},{16,0},{1,17},{17,1},{2,18},{18,2},{3,19},{19,3},{4,20},{20... | collective-permute-start | bytes 786440 | tf_op jit(solution)/shard_map/ppermute | solution.py:260
  34.0 0.2 lists.1.lists_ref
  34.2 0.9 collective-permute-done.1.columns_ref
  35.2 0.4 hidden.1
  35.6 19.2 %all_to_all.45.points_ref.own_points = bf16[8,128,256]{2,1,0:T(8,128)(2,1)S(1)} all-to-all(bf16[8,128,256]{2,1,0:T(8,128)(2,1)S(1)} %hidden.1), channel_id=1, replica_groups=mesh['x'=4,'yl'=2,'c'=2,'z'=8,'yh'=2] {'z'}, dimensions={0} | all-to-all | bytes 1048576 | tf_op jit(solution)/shard_map/all_to_all | solution.py:268
  54.8 1.7 %collective-permute-start.2 = (bf16[8,128,256]{2,1,0:T(8,128)(2,1)S(1)}, bf16[8,128,256]{2,1,0:T(8,128)(2,1)S(1)}, u32[]{:S(2)}, u32[]{:S(2)}) collective-permute-start(bf16[8,128,256]{2,1,0:T(8,128)(2,1)S(1)} %all_to_all.45.points_ref.own_points), channel_id=1, source_target_pairs={{0,16},{16,0},{1,17},{17,1},{2,18},{18,2},{3,19},{19,3},{4,20},{20... | collective-permute-start | bytes 1572872 | tf_op jit(solution)/shard_map/ppermute | solution.py:269
  56.5 1.3 first_energy.1
  57.9 0.2 collective-permute-done.2.points_ref.other_points
  58.0 1.4 second_energy.1
  59.4 12.0 %all_to_all.46.parts_ref = f32[16,8,128]{2,1,0:T(8,128)S(1)} all-to-all(f32[16,8,128]{2,1,0:T(8,128)S(1)} %get-tuple-element.17), channel_id=1, replica_groups=mesh['x'=4,'yl'=2,'c'=2,'z'=8,'yh'=2] {'yh','x','yl'}, dimensions={0} | all-to-all | bytes 131072 | tf_op jit(solution)/shard_map/all_to_all | solution.py:282
  71.4 0.7 row_sums.2
  72.1 11.4 %all_to_all.47.rows_ref = bf16[16,16,128]{2,1,0:T(8,128)(2,1)S(1)} all-to-all(bf16[16,16,128]{2,1,0:T(8,128)(2,1)S(1)} %row_sums.2), channel_id=1, replica_groups=mesh['x'=4,'yl'=2,'c'=2,'z'=8,'yh'=2] {'c','z'}, dimensions={0} | all-to-all | bytes 131072 | tf_op jit(solution)/shard_map/all_to_all | solution.py:284
  83.5 1.2 column_sums.2
  84.7 9.5 %all_to_all.48.parts_ref = f32[16,8,128]{2,1,0:T(8,128)S(1)} all-to-all(f32[16,8,128]{2,1,0:T(8,128)S(1)} %column_sums.2), channel_id=1, replica_groups=mesh['x'=4,'yl'=2,'c'=2,'z'=8,'yh'=2] {'yh','x','yl'}, dimensions={0} | all-to-all | bytes 131072 | tf_op jit(solution)/shard_map/all_to_all | solution.py:282
  94.2 0.7 row_sums.3.sent_ref
  94.9 11.9 %all_to_all.49.rows_ref = bf16[16,16,128]{2,1,0:T(8,128)(2,1)S(1)} all-to-all(bf16[16,16,128]{2,1,0:T(8,128)(2,1)S(1)} %row_sums.3.sent_ref), channel_id=1, replica_groups=mesh['x'=4,'yl'=2,'c'=2,'z'=8,'yh'=2] {'c','z'}, dimensions={0} | all-to-all | bytes 131072 | tf_op jit(solution)/shard_map/all_to_all | solution.py:284
  106.8 1.2 column_sums.3
  108.0 9.5 %all_to_all.50.parts_ref.columns_ref = f32[16,8,128]{2,1,0:T(8,128)S(1)} all-to-all(f32[16,8,128]{2,1,0:T(8,128)S(1)} %column_sums.3), channel_id=1, replica_groups=mesh['x'=4,'yl'=2,'c'=2,'z'=8,'yh'=2] {'yh','x','yl'}, dimensions={0} | all-to-all | bytes 131072 | tf_op jit(solution)/shard_map/all_to_all | solution.py:288
  117.5 0.7 row_change.1
  118.2 11.9 %all_to_all.51.change_ref = bf16[16,16,128]{2,1,0:T(8,128)(2,1)S(1)} all-to-all(bf16[16,16,128]{2,1,0:T(8,128)(2,1)S(1)} %row_change.1), channel_id=1, replica_groups=mesh['x'=4,'yl'=2,'c'=2,'z'=8,'yh'=2] {'c','z'}, dimensions={0} | all-to-all | bytes 131072 | tf_op jit(solution)/shard_map/all_to_all | solution.py:292
  130.1 2.2 %update.1 = (bf16[16,64,256]{2,1,0:T(8,128)(2,1)}, f32[8,128]{1,0:T(8,128)S(1)}) custom-call(s32[1]{0:T(128)} %bitcast.core_ref, bf16[16,16,128]{2,1,0:T(8,128)(2,1)S(1)} %all_to_all.49.rows_ref, bf16[16,16,128]{2,1,0:T(8,128)(2,1)S(1)} %all_to_all.51.change_ref, f32[16,8,128]{2,1,0:T(8,128)S(1)} %all_to_all.50.parts_ref.columns_ref, ...), custom_call_target="tpu_custom_call" | custom-call | tf_op jit(solution)/shard_map/update/pallas_call | solution.py:294
  132.3 3.6 %all-to-all-start.8 = ((bf16[16,64,256]{2,1,0:T(8,128)(2,1)}), bf16[16,64,256]{2,1,0:T(8,128)(2,1)S(1)}, u32[]{:S(2)}, u32[]{:S(2)}) async-start(bf16[16,64,256]{2,1,0:T(8,128)(2,1)} %get-tuple-element.20), calls=%async_computation.8 | async-start | bytes 1048576 | tf_op jit(solution)/shard_map/all_to_all | solution.py:297
  135.9 2.8 %collective-permute-start.3 = (f32[8,128]{1,0:T(8,128)S(1)}, f32[8,128]{1,0:T(8,128)S(1)}, u32[]{:S(2)}, u32[]{:S(2)}) collective-permute-start(f32[8,128]{1,0:T(8,128)S(1)} %get-tuple-element.21), channel_id=1, source_target_pairs={{0,1},{1,0},{2,3},{3,2},{4,5},{5,4},{6,7},{7,6},{8,9},{9,8},{10,11... | collective-permute-start | bytes 12296 | tf_op jit(solution)/shard_map/ppermute | solution.py:300
  138.7 1.9 %collective-permute-done.3 = f32[8,128]{1,0:T(8,128)S(1)} collective-permute-done((f32[8,128]{1,0:T(8,128)S(1)}, f32[8,128]{1,0:T(8,128)S(1)}, u32[]{:S(2)}, u32[]{:S(2)}) %collective-permute-start.3) | collective-permute-done | bytes 4128 | tf_op jit(solution)/shard_map/ppermute | solution.py:300
  140.6 0.6 copy.9
  141.2 5.3 %all-to-all-done.8.parts_ref = bf16[16,64,256]{2,1,0:T(8,128)(2,1)S(1)} async-done(((bf16[16,64,256]{2,1,0:T(8,128)(2,1)}), bf16[16,64,256]{2,1,0:T(8,128)(2,1)S(1)}, u32[]{:S(2)}, u32[]{:S(2)}) %all-to-all-start.8) | async-done | bytes 524320 | tf_op jit(solution)/shard_map/all_to_all | solution.py:297
  146.5 0.8 finish.1
  (4 shorter events, 0.1 us)
Async XLA Ops:
  0.6 13.7 %copy-start = (bf16[1024,256]{1,0:T(8,128)(2,1)S(1)}, bf16[1024,256]{1,0:T(8,128)(2,1)}, u32[]{:S(2)}) copy-start(bf16[1024,256]{1,0:T(8,128)(2,1)} %param.5) | copy-start | bytes 1572868
  2.5 28.9 %all-to-all-start = ((bf16[16,128,128]{2,1,0:T(8,128)(2,1)}), bf16[16,128,128]{2,1,0:T(8,128)(2,1)S(1)}, u32[]{:S(2)}, u32[]{:S(2)}) async-start(bf16[16,128,128]{2,1,0:T(8,128)(2,1)} %pack.1), calls=%async_computation | async-start | bytes 1048576 | tf_op jit(solution)/shard_map/all_to_all | solution.py:258
  14.3 9.5 %collective-permute-start = (bf16[512,256]{1,0:T(8,128)(2,1)S(1)}, bf16[512,256]{1,0:T(8,128)(2,1)S(1)}, u32[]{:S(2)}, u32[]{:S(2)}) collective-permute-start(bf16[512,256]{1,0:T(8,128)(2,1)S(1)} %bitcast.18), channel_id=1, source_target_pairs={{0,1},{1,0},{2,3},{3,2},{4,5},{5,4},{6,7},{7,6},{8,9},{9,8},{10,11... | collective-permute-start | bytes 786440 | tf_op jit(solution)/shard_map/ppermute | solution.py:244
  31.5 3.7 %collective-permute-start.1 = (bf16[16,64,128]{2,1,0:T(8,128)(2,1)S(1)}, bf16[16,64,128]{2,1,0:T(8,128)(2,1)S(1)}, u32[]{:S(2)}, u32[]{:S(2)}) collective-permute-start(bf16[16,64,128]{2,1,0:T(8,128)(2,1)S(1)} %slice.11), channel_id=1, source_target_pairs={{0,16},{16,0},{1,17},{17,1},{2,18},{18,2},{3,19},{19,3},{4,20},{20... | collective-permute-start | bytes 786440 | tf_op jit(solution)/shard_map/ppermute | solution.py:260
  54.8 3.3 %collective-permute-start.2 = (bf16[8,128,256]{2,1,0:T(8,128)(2,1)S(1)}, bf16[8,128,256]{2,1,0:T(8,128)(2,1)S(1)}, u32[]{:S(2)}, u32[]{:S(2)}) collective-permute-start(bf16[8,128,256]{2,1,0:T(8,128)(2,1)S(1)} %all_to_all.45.points_ref.own_points), channel_id=1, source_target_pairs={{0,16},{16,0},{1,17},{17,1},{2,18},{18,2},{3,19},{19,3},{4,20},{20... | collective-permute-start | bytes 1572872 | tf_op jit(solution)/shard_map/ppermute | solution.py:269
  132.3 14.2 %all-to-all-start.8 = ((bf16[16,64,256]{2,1,0:T(8,128)(2,1)}), bf16[16,64,256]{2,1,0:T(8,128)(2,1)S(1)}, u32[]{:S(2)}, u32[]{:S(2)}) async-start(bf16[16,64,256]{2,1,0:T(8,128)(2,1)} %get-tuple-element.20), calls=%async_computation.8 | async-start | bytes 1048576 | tf_op jit(solution)/shard_map/all_to_all | solution.py:297
  135.9 4.7 %collective-permute-start.3 = (f32[8,128]{1,0:T(8,128)S(1)}, f32[8,128]{1,0:T(8,128)S(1)}, u32[]{:S(2)}, u32[]{:S(2)}) collective-permute-start(f32[8,128]{1,0:T(8,128)S(1)} %get-tuple-element.21), channel_id=1, source_target_pairs={{0,1},{1,0},{2,3},{3,2},{4,5},{5,4},{6,7},{7,6},{8,9},{9,8},{10,11... | collective-permute-start | bytes 12296 | tf_op jit(solution)/shard_map/ppermute | solution.py:300

commit v7 on v6

--- a/solution.py
+++ b/solution.py
@@ -17,6 +17,7 @@
 SWAP = [(0, 1), (1, 0)]
 CHIPS = ("yh", "x", "yl")
 LISTS = ("c", "z")
+PLANE = ("yl", "yh", "x")
 bf16 = jnp.bfloat16
 f32 = jnp.float32
 VMEM = pltpu.VMEM
@@ -279,13 +280,13 @@
     sent_shape = shape((16, 16, 128), bf16)
     energies = (stay(own_energy), stay(other_energy))
     for sweep in range(ITERS - 1):
-        columns = lax.all_to_all(columns, CHIPS, 0, 0)
+        columns = lax.all_to_all(columns, PLANE, 0, 0)
         sent = call(row_kernel, sent_shape, "row_sums", 1, 3)(core_index, columns, *energies)
         rows = lax.all_to_all(sent, LISTS, 0, 0)
         columns = call(column_kernel, shape((16, 8, 128), f32), "column_sums", 1, 3)(
             core_index, rows, *energies
         )
-    columns = lax.all_to_all(columns, CHIPS, 0, 0)
+    columns = lax.all_to_all(columns, PLANE, 0, 0)
     change = call(change_kernel, sent_shape, "row_change", 1, 4)(
         core_index, columns, *energies, sent
     )

time: 148 us -> 148 us (level)
  no operation moved by 1% of the time
where the time goes in v7:
time: 148 us; the launch traced here: 147 us
  blocking collectives  85.2 us (58%)
  starting transfers between devices  25.4 us (17%)
  waiting for transfers between devices  22.5 us (15%)
  Pallas kernels  12.6 us (9%)
    all_to_all x3, blocking collectives, on_device(): columns = lax.all_to_all(columns, PLANE, 0, 0)  30.7 us
    all_to_all x2, blocking collectives, on_device(): rows = lax.all_to_all(sent, LISTS, 0, 0)  23.3 us
    all_to_all x1, blocking collectives, on_device(): points = lax.all_to_all(gathered, 'z', 0, 0)  19.2 us
    all_to_all x1, blocking collectives, on_device(): change = lax.all_to_all(change, LISTS, 0, 0)  11.9 us
    all_to_all x1, starting transfers between devices, on_device(): parts = lax.all_to_all(message, ('z', 'yh'), 0, 0)  11.8 us
    all_to_all x1, waiting for transfers between devices, on_device(): parts = lax.all_to_all(message, ('z', 'yh'), 0, 0)  7.56 us
    ppermute x1, waiting for transfers between devices, on_device(): taken = lax.ppermute(kept, 'yh', SWAP)  6.57 us
    all_to_all x1, waiting for transfers between devices, on_device(): owned = lax.all_to_all(sums, CHIPS, 0, 0)  5.32 us
  transfers between devices with their start and end apart: 6, of which 6 were waited for; matrix products, arithmetic and copies ran while one was open for 0% of the time, Pallas kernels for 1%

profile of v7, /device:TPU:1, one launch (start us, length us, event | category | flops | bytes accessed | tf_op | source)
XLA Modules:
  0.0 147.1 jit_solution(5996793866512822142)
XLA Ops:
  0.6 0.0 copy-start
  0.6 1.9 %pack.1 = bf16[16,128,128]{2,1,0:T(8,128)(2,1)} custom-call(s32[1]{0:T(128)} %bitcast.core_ref, bf16[64,2048]{1,0:T(8,128)(2,1)} %bitcast.21, bf16[64,256]{1,0:T(8,128)(2,1)} %projection_ref.1), custom_call_target="tpu_custom_call" | custom-call | tf_op jit(solution)/shard_map/pack/pallas_call | solution.py:246
  2.5 11.8 %all-to-all-start = ((bf16[16,128,128]{2,1,0:T(8,128)(2,1)}), bf16[16,128,128]{2,1,0:T(8,128)(2,1)S(1)}, u32[]{:S(2)}, u32[]{:S(2)}) async-start(bf16[16,128,128]{2,1,0:T(8,128)(2,1)} %pack.1), calls=%async_computation | async-start | bytes 1048576 | tf_op jit(solution)/shard_map/all_to_all | solution.py:259
  14.3 0.0 copy-done
  14.3 2.9 %collective-permute-start = (bf16[512,256]{1,0:T(8,128)(2,1)S(1)}, bf16[512,256]{1,0:T(8,128)(2,1)S(1)}, u32[]{:S(2)}, u32[]{:S(2)}) collective-permute-start(bf16[512,256]{1,0:T(8,128)(2,1)S(1)} %bitcast.18), channel_id=1, source_target_pairs={{0,1},{1,0},{2,3},{3,2},{4,5},{5,4},{6,7},{7,6},{8,9},{9,8},{10,11... | collective-permute-start | bytes 786440 | tf_op jit(solution)/shard_map/ppermute | solution.py:245
  17.3 6.6 %collective-permute-done.taken_ref = bf16[512,256]{1,0:T(8,128)(2,1)S(1)} collective-permute-done((bf16[512,256]{1,0:T(8,128)(2,1)S(1)}, bf16[512,256]{1,0:T(8,128)(2,1)S(1)}, u32[]{:S(2)}, u32[]{:S(2)}) %collective-permute-start) | collective-permute-done | bytes 262176 | tf_op jit(solution)/shard_map/ppermute | solution.py:245
  23.9 7.6 %all-to-all-done.parts_ref = bf16[16,128,128]{2,1,0:T(8,128)(2,1)S(1)} async-done(((bf16[16,128,128]{2,1,0:T(8,128)(2,1)}), bf16[16,128,128]{2,1,0:T(8,128)(2,1)S(1)}, u32[]{:S(2)}, u32[]{:S(2)}) %all-to-all-start) | async-done | bytes 524320 | tf_op jit(solution)/shard_map/all_to_all | solution.py:259
  31.5 2.6 %collective-permute-start.1 = (bf16[16,64,128]{2,1,0:T(8,128)(2,1)S(1)}, bf16[16,64,128]{2,1,0:T(8,128)(2,1)S(1)}, u32[]{:S(2)}, u32[]{:S(2)}) collective-permute-start(bf16[16,64,128]{2,1,0:T(8,128)(2,1)S(1)} %slice.11), channel_id=1, source_target_pairs={{0,16},{16,0},{1,17},{17,1},{2,18},{18,2},{3,19},{19,3},{4,20},{20... | collective-permute-start | bytes 786440 | tf_op jit(solution)/shard_map/ppermute | solution.py:261
  34.0 0.2 lists.1.lists_ref
  34.2 0.9 collective-permute-done.1.columns_ref
  35.2 0.4 hidden.1
  35.6 19.2 %all_to_all.45.points_ref.own_points = bf16[8,128,256]{2,1,0:T(8,128)(2,1)S(1)} all-to-all(bf16[8,128,256]{2,1,0:T(8,128)(2,1)S(1)} %hidden.1), channel_id=1, replica_groups=mesh['x'=4,'yl'=2,'c'=2,'z'=8,'yh'=2] {'z'}, dimensions={0} | all-to-all | bytes 1048576 | tf_op jit(solution)/shard_map/all_to_all | solution.py:269
  54.8 1.7 %collective-permute-start.2 = (bf16[8,128,256]{2,1,0:T(8,128)(2,1)S(1)}, bf16[8,128,256]{2,1,0:T(8,128)(2,1)S(1)}, u32[]{:S(2)}, u32[]{:S(2)}) collective-permute-start(bf16[8,128,256]{2,1,0:T(8,128)(2,1)S(1)} %all_to_all.45.points_ref.own_points), channel_id=1, source_target_pairs={{0,16},{16,0},{1,17},{17,1},{2,18},{18,2},{3,19},{19,3},{4,20},{20... | collective-permute-start | bytes 1572872 | tf_op jit(solution)/shard_map/ppermute | solution.py:270
  56.5 1.3 first_energy.1
  57.9 0.2 collective-permute-done.2.points_ref.other_points
  58.0 1.4 second_energy.1
  59.4 12.1 %all_to_all.46.parts_ref = f32[16,8,128]{2,1,0:T(8,128)S(1)} all-to-all(f32[16,8,128]{2,1,0:T(8,128)S(1)} %get-tuple-element.17), channel_id=1, replica_groups=mesh['x'=4,'yl'=2,'c'=2,'z'=8,'yh'=2] {'yl','yh','x'}, dimensions={0} | all-to-all | bytes 131072 | tf_op jit(solution)/shard_map/all_to_all | solution.py:283
  71.5 0.7 row_sums.2
  72.2 11.4 %all_to_all.47.rows_ref = bf16[16,16,128]{2,1,0:T(8,128)(2,1)S(1)} all-to-all(bf16[16,16,128]{2,1,0:T(8,128)(2,1)S(1)} %row_sums.2), channel_id=1, replica_groups=mesh['x'=4,'yl'=2,'c'=2,'z'=8,'yh'=2] {'c','z'}, dimensions={0} | all-to-all | bytes 131072 | tf_op jit(solution)/shard_map/all_to_all | solution.py:285
  83.6 1.2 column_sums.2
  84.8 9.3 %all_to_all.48.parts_ref = f32[16,8,128]{2,1,0:T(8,128)S(1)} all-to-all(f32[16,8,128]{2,1,0:T(8,128)S(1)} %column_sums.2), channel_id=1, replica_groups=mesh['x'=4,'yl'=2,'c'=2,'z'=8,'yh'=2] {'yl','yh','x'}, dimensions={0} | all-to-all | bytes 131072 | tf_op jit(solution)/shard_map/all_to_all | solution.py:283
  94.1 0.7 row_sums.3.sent_ref
  94.8 11.9 %all_to_all.49.rows_ref = bf16[16,16,128]{2,1,0:T(8,128)(2,1)S(1)} all-to-all(bf16[16,16,128]{2,1,0:T(8,128)(2,1)S(1)} %row_sums.3.sent_ref), channel_id=1, replica_groups=mesh['x'=4,'yl'=2,'c'=2,'z'=8,'yh'=2] {'c','z'}, dimensions={0} | all-to-all | bytes 131072 | tf_op jit(solution)/shard_map/all_to_all | solution.py:285
  106.7 1.2 column_sums.3
  107.9 9.3 %all_to_all.50.parts_ref.columns_ref = f32[16,8,128]{2,1,0:T(8,128)S(1)} all-to-all(f32[16,8,128]{2,1,0:T(8,128)S(1)} %column_sums.3), channel_id=1, replica_groups=mesh['x'=4,'yl'=2,'c'=2,'z'=8,'yh'=2] {'yl','yh','x'}, dimensions={0} | all-to-all | bytes 131072 | tf_op jit(solution)/shard_map/all_to_all | solution.py:289
  117.3 0.7 row_change.1
  117.9 11.9 %all_to_all.51.change_ref = bf16[16,16,128]{2,1,0:T(8,128)(2,1)S(1)} all-to-all(bf16[16,16,128]{2,1,0:T(8,128)(2,1)S(1)} %row_change.1), channel_id=1, replica_groups=mesh['x'=4,'yl'=2,'c'=2,'z'=8,'yh'=2] {'c','z'}, dimensions={0} | all-to-all | bytes 131072 | tf_op jit(solution)/shard_map/all_to_all | solution.py:293
  129.9 2.2 %update.1 = (bf16[16,64,256]{2,1,0:T(8,128)(2,1)}, f32[8,128]{1,0:T(8,128)S(1)}) custom-call(s32[1]{0:T(128)} %bitcast.core_ref, bf16[16,16,128]{2,1,0:T(8,128)(2,1)S(1)} %all_to_all.49.rows_ref, bf16[16,16,128]{2,1,0:T(8,128)(2,1)S(1)} %all_to_all.51.change_ref, f32[16,8,128]{2,1,0:T(8,128)S(1)} %all_to_all.50.parts_ref.columns_ref, ...), custom_call_target="tpu_custom_call" | custom-call | tf_op jit(solution)/shard_map/update/pallas_call | solution.py:295
  132.1 3.6 %all-to-all-start.8 = ((bf16[16,64,256]{2,1,0:T(8,128)(2,1)}), bf16[16,64,256]{2,1,0:T(8,128)(2,1)S(1)}, u32[]{:S(2)}, u32[]{:S(2)}) async-start(bf16[16,64,256]{2,1,0:T(8,128)(2,1)} %get-tuple-element.20), calls=%async_computation.8 | async-start | bytes 1048576 | tf_op jit(solution)/shard_map/all_to_all | solution.py:298
  135.7 2.8 %collective-permute-start.3 = (f32[8,128]{1,0:T(8,128)S(1)}, f32[8,128]{1,0:T(8,128)S(1)}, u32[]{:S(2)}, u32[]{:S(2)}) collective-permute-start(f32[8,128]{1,0:T(8,128)S(1)} %get-tuple-element.21), channel_id=1, source_target_pairs={{0,1},{1,0},{2,3},{3,2},{4,5},{5,4},{6,7},{7,6},{8,9},{9,8},{10,11... | collective-permute-start | bytes 12296 | tf_op jit(solution)/shard_map/ppermute | solution.py:301
  138.5 1.9 %collective-permute-done.3 = f32[8,128]{1,0:T(8,128)S(1)} collective-permute-done((f32[8,128]{1,0:T(8,128)S(1)}, f32[8,128]{1,0:T(8,128)S(1)}, u32[]{:S(2)}, u32[]{:S(2)}) %collective-permute-start.3) | collective-permute-done | bytes 4128 | tf_op jit(solution)/shard_map/ppermute | solution.py:301
  140.4 0.6 copy.9
  141.0 5.3 %all-to-all-done.8.parts_ref = bf16[16,64,256]{2,1,0:T(8,128)(2,1)S(1)} async-done(((bf16[16,64,256]{2,1,0:T(8,128)(2,1)}), bf16[16,64,256]{2,1,0:T(8,128)(2,1)S(1)}, u32[]{:S(2)}, u32[]{:S(2)}) %all-to-all-start.8) | async-done | bytes 524320 | tf_op jit(solution)/shard_map/all_to_all | solution.py:298
  146.3 0.8 finish.1
  (4 shorter events, 0.1 us)
Async XLA Ops:
  0.6 13.7 %copy-start = (bf16[1024,256]{1,0:T(8,128)(2,1)S(1)}, bf16[1024,256]{1,0:T(8,128)(2,1)}, u32[]{:S(2)}) copy-start(bf16[1024,256]{1,0:T(8,128)(2,1)} %param.5) | copy-start | bytes 1572868
  2.5 28.9 %all-to-all-start = ((bf16[16,128,128]{2,1,0:T(8,128)(2,1)}), bf16[16,128,128]{2,1,0:T(8,128)(2,1)S(1)}, u32[]{:S(2)}, u32[]{:S(2)}) async-start(bf16[16,128,128]{2,1,0:T(8,128)(2,1)} %pack.1), calls=%async_computation | async-start | bytes 1048576 | tf_op jit(solution)/shard_map/all_to_all | solution.py:259
  14.3 9.5 %collective-permute-start = (bf16[512,256]{1,0:T(8,128)(2,1)S(1)}, bf16[512,256]{1,0:T(8,128)(2,1)S(1)}, u32[]{:S(2)}, u32[]{:S(2)}) collective-permute-start(bf16[512,256]{1,0:T(8,128)(2,1)S(1)} %bitcast.18), channel_id=1, source_target_pairs={{0,1},{1,0},{2,3},{3,2},{4,5},{5,4},{6,7},{7,6},{8,9},{9,8},{10,11... | collective-permute-start | bytes 786440 | tf_op jit(solution)/shard_map/ppermute | solution.py:245
  31.5 3.7 %collective-permute-start.1 = (bf16[16,64,128]{2,1,0:T(8,128)(2,1)S(1)}, bf16[16,64,128]{2,1,0:T(8,128)(2,1)S(1)}, u32[]{:S(2)}, u32[]{:S(2)}) collective-permute-start(bf16[16,64,128]{2,1,0:T(8,128)(2,1)S(1)} %slice.11), channel_id=1, source_target_pairs={{0,16},{16,0},{1,17},{17,1},{2,18},{18,2},{3,19},{19,3},{4,20},{20... | collective-permute-start | bytes 786440 | tf_op jit(solution)/shard_map/ppermute | solution.py:261
  54.8 3.3 %collective-permute-start.2 = (bf16[8,128,256]{2,1,0:T(8,128)(2,1)S(1)}, bf16[8,128,256]{2,1,0:T(8,128)(2,1)S(1)}, u32[]{:S(2)}, u32[]{:S(2)}) collective-permute-start(bf16[8,128,256]{2,1,0:T(8,128)(2,1)S(1)} %all_to_all.45.points_ref.own_points), channel_id=1, source_target_pairs={{0,16},{16,0},{1,17},{17,1},{2,18},{18,2},{3,19},{19,3},{4,20},{20... | collective-permute-start | bytes 1572872 | tf_op jit(solution)/shard_map/ppermute | solution.py:270
  132.1 14.2 %all-to-all-start.8 = ((bf16[16,64,256]{2,1,0:T(8,128)(2,1)}), bf16[16,64,256]{2,1,0:T(8,128)(2,1)S(1)}, u32[]{:S(2)}, u32[]{:S(2)}) async-start(bf16[16,64,256]{2,1,0:T(8,128)(2,1)} %get-tuple-element.20), calls=%async_computation.8 | async-start | bytes 1048576 | tf_op jit(solution)/shard_map/all_to_all | solution.py:298
  135.7 4.7 %collective-permute-start.3 = (f32[8,128]{1,0:T(8,128)S(1)}, f32[8,128]{1,0:T(8,128)S(1)}, u32[]{:S(2)}, u32[]{:S(2)}) collective-permute-start(f32[8,128]{1,0:T(8,128)S(1)} %get-tuple-element.21), channel_id=1, source_target_pairs={{0,1},{1,0},{2,3},{3,2},{4,5},{5,4},{6,7},{7,6},{8,9},{9,8},{10,11... | collective-permute-start | bytes 12296 | tf_op jit(solution)/shard_map/ppermute | solution.py:301
